TPU v7x, 32 devices: a whole 2x2x4 slice. The times are simulated.
32 devices in a mesh: wide: 8 (over z, x), narrow: 4 (over y, core).
Axes of the slice: x: 2, y: 2, z: 4, core: 2. Of those that a mesh axis runs over, the one named last changes fastest.
Arguments:
- block_input: float32 [16384, 1152], P('wide', 'narrow'), may hold values from -6 to 6
- condition: float32 [4, 1152], replicated, may hold values from -6 to 6
- frame_counts: int32 [4], replicated, may hold values from 8 to 16, as said below
- cotangent: float32 [16384, 1152], P('wide', 'narrow'), may hold values from -6 to 6
- qkv_weight: float32 [2, 1152, 3, 1152], P(None, 'wide', None, 'narrow'), may hold values from -0.23570226 to 0.23570226
- qkv_first: float32 [2, 1152, 3, 1152], P(None, 'wide', None, 'narrow'), may hold values from -0.00021362305 to 0.00021362305
- qkv_second: float32 [2, 1152, 3, 1152], P(None, 'wide', None, 'narrow'), may hold values from 2.0917e-11 to 8.3668e-11
- out_weight: float32 [2, 1152, 1152], P(None, 'wide', 'narrow'), may hold values from -0.94280904 to 0.94280904
- out_first: float32 [2, 1152, 1152], P(None, 'wide', 'narrow'), may hold values from -0.00021362305 to 0.00021362305
- out_second: float32 [2, 1152, 1152], P(None, 'wide', 'narrow'), may hold values from 2.0917e-11 to 8.3668e-11
- up_weight: float32 [2, 1152, 4, 1152], P(None, 'wide', None, 'narrow'), may hold values from -0.23570226 to 0.23570226
- up_first: float32 [2, 1152, 4, 1152], P(None, 'wide', None, 'narrow'), may hold values from -0.00021362305 to 0.00021362305
- up_second: float32 [2, 1152, 4, 1152], P(None, 'wide', None, 'narrow'), may hold values from 2.0917e-11 to 8.3668e-11
- down_weight: float32 [2, 1152, 4, 1152], P(None, 'wide', None, 'narrow'), may hold values from -0.11785113 to 0.11785113
- down_first: float32 [2, 1152, 4, 1152], P(None, 'wide', None, 'narrow'), may hold values from -0.00021362305 to 0.00021362305
- down_second: float32 [2, 1152, 4, 1152], P(None, 'wide', None, 'narrow'), may hold values from 2.0917e-11 to 8.3668e-11
- ada_weight: float32 [2, 1152, 6, 1152], P(None, 'wide', None, 'narrow'), may hold values from -0.23570226 to 0.23570226
- ada_first: float32 [2, 1152, 6, 1152], P(None, 'wide', None, 'narrow'), may hold values from -0.00021362305 to 0.00021362305
- ada_second: float32 [2, 1152, 6, 1152], P(None, 'wide', None, 'narrow'), may hold values from 2.0917e-11 to 8.3668e-11
- bias_weight: float32 [2, 14, 1152], P(None, None, 'narrow'), may hold values from -4 to 4
- bias_first: float32 [2, 14, 1152], P(None, None, 'narrow'), may hold values from -0.00061035156 to 0.00061035156
- bias_second: float32 [2, 14, 1152], P(None, None, 'narrow'), may hold values from 2.0917001e-10 to 8.3668006e-10
Outputs:
- block_output: float32 [16384, 1152], P('wide', 'narrow')
- input_grad: float32 [16384, 1152], P('wide', 'narrow')
- qkv_next: float32 [2, 1152, 3, 1152], P(None, 'wide', None, 'narrow')
- qkv_moment: float32 [2, 1152, 3, 1152], P(None, 'wide', None, 'narrow')
- qkv_square: float32 [2, 1152, 3, 1152], P(None, 'wide', None, 'narrow')
- out_next: float32 [2, 1152, 1152], P(None, 'wide', 'narrow')
- out_moment: float32 [2, 1152, 1152], P(None, 'wide', 'narrow')
- out_square: float32 [2, 1152, 1152], P(None, 'wide', 'narrow')
- up_next: float32 [2, 1152, 4, 1152], P(None, 'wide', None, 'narrow')
- up_moment: float32 [2, 1152, 4, 1152], P(None, 'wide', None, 'narrow')
- up_square: float32 [2, 1152, 4, 1152], P(None, 'wide', None, 'narrow')
- down_next: float32 [2, 1152, 4, 1152], P(None, 'wide', None, 'narrow')
- down_moment: float32 [2, 1152, 4, 1152], P(None, 'wide', None, 'narrow')
- down_square: float32 [2, 1152, 4, 1152], P(None, 'wide', None, 'narrow')
- ada_next: float32 [2, 1152, 6, 1152], P(None, 'wide', None, 'narrow')
- ada_moment: float32 [2, 1152, 6, 1152], P(None, 'wide', None, 'narrow')
- ada_square: float32 [2, 1152, 6, 1152], P(None, 'wide', None, 'narrow')
- bias_next: float32 [2, 14, 1152], P(None, None, 'narrow')
- bias_moment: float32 [2, 14, 1152], P(None, None, 'narrow')
- bias_square: float32 [2, 14, 1152], P(None, None, 'narrow')
- trust_norms: float32 [2, 6, 2], replicated
- grad_norm: float32 [1], replicated
Inputs may be any that keep to these rules, and one draw needn't show every extreme that they name: Clip c holds frame_counts[c] frames of data at its first positions, the rest of its 16 frames are padding that no token attends to; some clip holds 16 frames.
All inputs are finite; a program needn't handle non-finite values.
Results may differ from a plain program's by a relative error of at most 0.04.
Values may be sent and summed in bfloat16 or wider, within the bound.
A program may use at most 320 MiB of HBM per device.

v0:
```python
import jax
import jax.numpy as jnp
from jax import lax
from jax.sharding import PartitionSpec as P

HEAD_DIM = 72
PATCHES = 256
CLIP_LEN = 16
STEP = 10


HIGHEST_PREC = lax.Precision.HIGHEST
NORM_EPS = 1e-06
BETA_ONE = 0.9
BETA_TWO = 0.999
ADAM_EPS = 1e-06
WEIGHT_DECAY = 0.01
LEARN_RATE = 0.5
CLIP_LIMIT = 1.0
MASKED = -1e30


def whole_rows(fragment):
    return lax.all_gather(fragment, "narrow", axis=2, tiled=True)


def sum_columns(partial_sum):
    return lax.psum_scatter(
        partial_sum.astype(jnp.bfloat16), "narrow", scatter_dimension=2, tiled=True
    ).astype(jnp.float32)


def to_patches(stacked):
    return lax.all_to_all(stacked, "wide", split_axis=2, concat_axis=1, tiled=True)


def to_frames(stacked):
    return lax.all_to_all(stacked, "wide", split_axis=1, concat_axis=2, tiled=True)


def fetch_rows(weight_tiles):
    return (
        lax.all_gather(weight_tiles[0], "wide", axis=0, tiled=True),
        lax.all_gather(weight_tiles[1], "wide", axis=0, tiled=True),
        lax.all_gather(weight_tiles[2], "wide", axis=0, tiled=True),
        lax.all_gather(weight_tiles[3], "wide", axis=0, tiled=True),
    )


def fetch_again(weight_tiles):
    return (
        lax.all_gather(weight_tiles[0], "wide", axis=0, tiled=True),
        lax.all_gather(weight_tiles[1], "wide", axis=0, tiled=True),
        lax.all_gather(weight_tiles[2], "wide", axis=0, tiled=True),
        lax.all_gather(weight_tiles[3], "wide", axis=0, tiled=True),
    )


def own_cols(full_rows, col_start, col_width):
    return lax.dynamic_slice_in_dim(full_rows, col_start, col_width, full_rows.ndim - 1)


def normalize(full_rows):
    row_mean = jnp.mean(full_rows, axis=-1, keepdims=True)
    centered = full_rows - row_mean
    inverse = lax.rsqrt(jnp.mean(centered * centered, axis=-1, keepdims=True) + NORM_EPS)
    return (centered * inverse, inverse)


def norm_modulate(residual, shift_vec, scale_vec):
    full_rows = whole_rows(residual.astype(jnp.bfloat16)).astype(jnp.float32)
    normed, inverse = normalize(full_rows)
    hidden = (normed * (1.0 + scale_vec) + shift_vec).astype(jnp.bfloat16)
    return (normed, inverse, hidden)


def arrange(stacked, temporal):
    members, frames_all, patches_here, col_width = stacked.shape
    head_count = col_width // HEAD_DIM
    if temporal:
        clip_total = frames_all // CLIP_LEN
        shaped = stacked.reshape(members, clip_total, CLIP_LEN, patches_here, head_count, HEAD_DIM)
        shaped = jnp.transpose(shaped, (0, 1, 3, 2, 4, 5))
        return shaped.reshape(members, clip_total * patches_here, CLIP_LEN, head_count, HEAD_DIM)
    return stacked.reshape(members, frames_all, patches_here, head_count, HEAD_DIM)


def unarrange(arranged, patches_here, temporal):
    members, batch_rows, length, head_count, head_width = arranged.shape
    if temporal:
        clip_total = batch_rows // patches_here
        shaped = arranged.reshape(members, clip_total, patches_here, length, head_count, head_width)
        shaped = jnp.transpose(shaped, (0, 1, 3, 2, 4, 5))
        return shaped.reshape(members, clip_total * length, patches_here, head_count * head_width)
    return arranged.reshape(members, batch_rows, length, head_count * head_width)


def masked_scores(queries, key_rows, key_mask):
    head_scale = queries.shape[-1] ** (-0.5)
    scores = (
        jnp.einsum("blhe,bmhe->bhlm", queries, key_rows, preferred_element_type=jnp.float32)
        * head_scale
    )
    return (jnp.where(key_mask[:, None, None, :], scores, MASKED), head_scale)


def attend_forward(queries, key_rows, value_rows, key_mask):
    scores, head_scale = masked_scores(queries, key_rows, key_mask)
    row_max = jnp.max(scores, axis=-1, keepdims=True)
    raised = jnp.exp(scores - row_max)
    summed = jnp.sum(raised, axis=-1, keepdims=True)
    attn_probs = (raised / summed).astype(jnp.bfloat16)
    outputs = jnp.einsum(
        "bhlm,bmhe->blhe", attn_probs, value_rows, preferred_element_type=jnp.float32
    )
    return (outputs.astype(jnp.bfloat16), (row_max, summed))


def attend_backward(queries, key_rows, value_rows, key_mask, softmax_stats, grad_outputs):
    row_max, summed = softmax_stats
    scores, head_scale = masked_scores(queries, key_rows, key_mask)
    attn_probs = jnp.exp(scores - row_max) / summed
    grad_probs = jnp.einsum(
        "blhe,bmhe->bhlm", grad_outputs, value_rows, preferred_element_type=jnp.float32
    )
    row_delta = jnp.sum(grad_probs * attn_probs, axis=-1, keepdims=True)
    grad_scores = (attn_probs * (grad_probs - row_delta)).astype(jnp.bfloat16)
    grad_queries = (
        jnp.einsum("bhlm,bmhe->blhe", grad_scores, key_rows, preferred_element_type=jnp.float32)
        * head_scale
    ).astype(jnp.bfloat16)
    grad_keys = (
        jnp.einsum("bhlm,blhe->bmhe", grad_scores, queries, preferred_element_type=jnp.float32)
        * head_scale
    ).astype(jnp.bfloat16)
    grad_values = jnp.einsum(
        "bhlm,blhe->bmhe",
        attn_probs.astype(jnp.bfloat16),
        grad_outputs,
        preferred_element_type=jnp.float32,
    ).astype(jnp.bfloat16)
    return (grad_queries, grad_keys, grad_values)


def attention_forward(qkv_rows, temporal, key_mask):
    moved = to_patches(qkv_rows) if temporal else qkv_rows
    patches_here = moved.shape[2]
    arranged = arrange(moved, temporal)
    outputs, softmax_stats = attend_forward(arranged[0], arranged[1], arranged[2], key_mask)
    heads_out = unarrange(outputs[None], patches_here, temporal)
    if temporal:
        heads_out = to_frames(heads_out)
    return (heads_out[0], (arranged, softmax_stats))


def attention_backward(grad_heads, kept_attn, temporal, key_mask):
    arranged, softmax_stats = kept_attn
    moved = to_patches(grad_heads[None]) if temporal else grad_heads[None]
    grad_arranged = arrange(moved, temporal)[0]
    grad_parts = attend_backward(
        arranged[0], arranged[1], arranged[2], key_mask, softmax_stats, grad_arranged
    )
    stacked = unarrange(jnp.stack(grad_parts), moved.shape[2], temporal)
    return to_frames(stacked) if temporal else stacked


def norm_backward(partial_sum, normed, inverse, scale_vec, col_start, col_width):
    full_width = normed.shape[-1]
    normed_own = own_cols(normed, col_start, col_width)
    grad_hidden = lax.psum_scatter(
        partial_sum.astype(jnp.bfloat16), "narrow", scatter_dimension=2, tiled=True
    ).astype(jnp.float32)
    grad_normed = grad_hidden * (1.0 + own_cols(scale_vec, col_start, col_width))
    row_first, row_second = lax.psum(
        (
            jnp.sum(grad_normed, axis=-1, keepdims=True),
            jnp.sum(grad_normed * normed_own, axis=-1, keepdims=True),
        ),
        "narrow",
    )
    grad_input = inverse * (
        grad_normed - row_first / full_width - normed_own * (row_second / full_width)
    )
    grad_shift = jnp.sum(grad_hidden, axis=1)
    grad_scale = jnp.sum(grad_hidden * normed_own, axis=1)
    return (grad_input, grad_shift, grad_scale)


def modulations(modul, col_start, col_width):
    shift_one = modul[:, 0][:, None, :]
    scale_one = modul[:, 1][:, None, :]
    gate_one = own_cols(modul[:, 2], col_start, col_width)[:, None, :]
    shift_two = modul[:, 3][:, None, :]
    scale_two = modul[:, 4][:, None, :]
    gate_two = own_cols(modul[:, 5], col_start, col_width)[:, None, :]
    return (shift_one, scale_one, gate_one, shift_two, scale_two, gate_two)


def forward_block(
    residual, modul, weight_rows, bias_rows, temporal, key_mask, col_start, col_width
):
    w_qkv, w_out, w_up, w_down = weight_rows
    expand = w_up.shape[1]
    shift_one, scale_one, gate_one, shift_two, scale_two, gate_two = modulations(
        modul, col_start, col_width
    )
    normed_one, inverse_one, hidden_one = norm_modulate(residual, shift_one, scale_one)
    qkv_bias = jnp.stack([bias_rows[0], jnp.zeros_like(bias_rows[0]), bias_rows[1]])
    qkv_rows = (
        jnp.einsum("fpd,dke->kfpe", hidden_one, w_qkv, preferred_element_type=jnp.float32)
        + qkv_bias[:, None, None, :]
    ).astype(jnp.bfloat16)
    heads_out, kept_attn = attention_forward(qkv_rows, temporal, key_mask)
    attn_branch = (
        sum_columns(jnp.einsum("fpe,de->fpd", heads_out, w_out, preferred_element_type=jnp.float32))
        + bias_rows[2]
    )
    middle = residual + gate_one * attn_branch
    normed_two, inverse_two, hidden_two = norm_modulate(middle, shift_two, scale_two)
    upper = (
        jnp.einsum("fpd,dke->fpke", hidden_two, w_up, preferred_element_type=jnp.float32)
        + bias_rows[3 : 3 + expand]
    )
    active = jax.nn.gelu(upper, approximate=True).astype(jnp.bfloat16)
    mlp_branch = (
        sum_columns(jnp.einsum("fpke,dke->fpd", active, w_down, preferred_element_type=jnp.float32))
        + bias_rows[3 + expand]
    )
    output = middle + gate_two * mlp_branch
    kept_vals = (
        normed_one,
        inverse_one,
        hidden_one,
        heads_out,
        kept_attn,
        attn_branch,
        normed_two,
        inverse_two,
        hidden_two,
        upper,
        active,
        mlp_branch,
    )
    return (output, kept_vals)


def backward_block(
    grad_out, kept_vals, modul, weight_rows, temporal, key_mask, col_start, col_width
):
    (
        normed_one,
        inverse_one,
        hidden_one,
        heads_out,
        kept_attn,
        attn_branch,
        normed_two,
        inverse_two,
        hidden_two,
        upper,
        active,
        mlp_branch,
    ) = kept_vals
    w_qkv, w_out, w_up, w_down = weight_rows
    shift_one, scale_one, gate_one, shift_two, scale_two, gate_two = modulations(
        modul, col_start, col_width
    )
    grad_mlp = (grad_out * gate_two).astype(jnp.bfloat16)
    grad_gate_two = jnp.sum(grad_out * mlp_branch, axis=1)
    grad_mlp_rows = whole_rows(grad_mlp)
    grad_down = jnp.einsum(
        "fpd,fpke->dke", grad_mlp_rows, active, preferred_element_type=jnp.float32
    )
    grad_active = jnp.einsum(
        "fpd,dke->fpke", grad_mlp_rows, w_down, preferred_element_type=jnp.float32
    )
    gelu_pull = jax.vjp(lambda value_in: jax.nn.gelu(value_in, approximate=True), upper)[1]
    grad_upper = gelu_pull(grad_active)[0].astype(jnp.bfloat16)
    grad_up = jnp.einsum(
        "fpd,fpke->dke", hidden_two, grad_upper, preferred_element_type=jnp.float32
    )
    grad_norm_two, grad_shift_two, grad_scale_two = norm_backward(
        jnp.einsum("fpke,dke->fpd", grad_upper, w_up, preferred_element_type=jnp.float32),
        normed_two,
        inverse_two,
        scale_two,
        col_start,
        col_width,
    )
    grad_middle = grad_out + grad_norm_two
    grad_attn = (grad_middle * gate_one).astype(jnp.bfloat16)
    grad_gate_one = jnp.sum(grad_middle * attn_branch, axis=1)
    grad_attn_rows = whole_rows(grad_attn)
    grad_out_weight = jnp.einsum(
        "fpd,fpe->de", grad_attn_rows, heads_out, preferred_element_type=jnp.float32
    )
    grad_heads = jnp.einsum(
        "fpd,de->fpe", grad_attn_rows, w_out, preferred_element_type=jnp.float32
    ).astype(jnp.bfloat16)
    grad_qkv = attention_backward(grad_heads, kept_attn, temporal, key_mask)
    grad_qkv_weight = jnp.einsum(
        "fpd,kfpe->dke", hidden_one, grad_qkv, preferred_element_type=jnp.float32
    )
    grad_norm_one, grad_shift_one, grad_scale_one = norm_backward(
        jnp.einsum("kfpe,dke->fpd", grad_qkv, w_qkv, preferred_element_type=jnp.float32),
        normed_one,
        inverse_one,
        scale_one,
        col_start,
        col_width,
    )
    grad_input = grad_middle + grad_norm_one
    tile_grads = (
        lax.psum_scatter(
            grad_qkv_weight.astype(jnp.bfloat16), "wide", scatter_dimension=0, tiled=True
        ).astype(jnp.float32),
        lax.psum_scatter(
            grad_out_weight.astype(jnp.bfloat16), "wide", scatter_dimension=0, tiled=True
        ).astype(jnp.float32),
        lax.psum_scatter(
            grad_up.astype(jnp.bfloat16), "wide", scatter_dimension=0, tiled=True
        ).astype(jnp.float32),
        lax.psum_scatter(
            grad_down.astype(jnp.bfloat16), "wide", scatter_dimension=0, tiled=True
        ).astype(jnp.float32),
    )
    grad_frames = jnp.stack(
        [
            grad_shift_one,
            grad_scale_one,
            grad_gate_one,
            grad_shift_two,
            grad_scale_two,
            grad_gate_two,
        ],
        axis=1,
    )
    qkv_sums = jnp.sum(grad_qkv, axis=(1, 2), dtype=jnp.float32)
    grad_lin = jnp.concatenate(
        [
            qkv_sums[0:1],
            qkv_sums[2:3],
            jnp.sum(grad_attn, axis=(0, 1), dtype=jnp.float32)[None],
            jnp.sum(grad_upper, axis=(0, 1), dtype=jnp.float32),
            jnp.sum(grad_mlp, axis=(0, 1), dtype=jnp.float32)[None],
        ],
        axis=0,
    )
    return (grad_input, grad_frames, grad_lin, tile_grads)


def on_device(
    block_input,
    condition,
    frame_counts,
    cotangent,
    qkv_weight,
    qkv_first,
    qkv_second,
    out_weight,
    out_first,
    out_second,
    up_weight,
    up_first,
    up_second,
    down_weight,
    down_first,
    down_second,
    ada_weight,
    ada_first,
    ada_second,
    bias_weight,
    bias_first,
    bias_second,
):
    wide_count = lax.axis_size("wide")
    narrow_count = lax.axis_size("narrow")
    wide_at = lax.axis_index("wide")
    narrow_at = lax.axis_index("narrow")
    frames = block_input.shape[0] // PATCHES
    clip_total = condition.shape[0]
    col_width = block_input.shape[1]
    rows_tile = qkv_weight.shape[1]
    expand = up_weight.shape[2]
    full_width = col_width * narrow_count
    col_start = narrow_at * col_width
    silu_cond = jax.nn.silu(condition)
    cond_rows = lax.dynamic_slice_in_dim(silu_cond, wide_at * rows_tile, rows_tile, 1)
    partial_mod = jnp.einsum("cd,ldke->lcke", cond_rows, ada_weight, precision=HIGHEST_PREC)
    ada_bias = bias_weight[:, 4 + expand : 10 + expand]
    partial_mod = partial_mod + jnp.where(wide_at == 0, ada_bias, jnp.zeros_like(ada_bias))[:, None]
    zero_at = jnp.zeros((), jnp.int32)
    padded = lax.dynamic_update_slice(
        jnp.zeros((2, clip_total, 6, full_width), jnp.float32),
        partial_mod,
        (zero_at, zero_at, zero_at, col_start),
    )
    modul_all = lax.psum(padded, ("wide", "narrow"))
    frame_ids = wide_at * frames + jnp.arange(frames, dtype=jnp.int32)
    pick = (
        frame_ids[:, None] // CLIP_LEN == jnp.arange(clip_total, dtype=jnp.int32)[None, :]
    ).astype(jnp.float32)
    frame_mod = jnp.einsum("fc,lcke->lfke", pick, modul_all, precision=HIGHEST_PREC)
    patch_width = PATCHES // wide_count
    valid = jnp.arange(CLIP_LEN, dtype=jnp.int32)[None, :] < frame_counts[:, None]
    temporal_mask = jnp.broadcast_to(
        valid[:, None, :], (clip_total, patch_width, CLIP_LEN)
    ).reshape(clip_total * patch_width, CLIP_LEN)
    spatial_mask = jnp.ones((frames, PATCHES), dtype=bool)
    masks = (spatial_mask, temporal_mask)
    low_tiles = [
        (
            qkv_weight[layer_idx].astype(jnp.bfloat16),
            out_weight[layer_idx].astype(jnp.bfloat16),
            up_weight[layer_idx].astype(jnp.bfloat16),
            down_weight[layer_idx].astype(jnp.bfloat16),
        )
        for layer_idx in range(2)
    ]
    residual = block_input.reshape(frames, PATCHES, col_width)
    gathered = [None, None]
    kept = [None, None]
    for layer_idx in range(2):
        gathered[layer_idx] = fetch_rows(low_tiles[layer_idx])
        residual, kept[layer_idx] = forward_block(
            residual,
            frame_mod[layer_idx],
            gathered[layer_idx],
            bias_weight[layer_idx],
            layer_idx == 1,
            masks[layer_idx],
            col_start,
            col_width,
        )
    block_output = residual.reshape(frames * PATCHES, col_width)
    grad_state = cotangent.reshape(frames, PATCHES, col_width)
    frame_grads = [None, None]
    bias_grads = [None, None]
    tile_grads = [None, None]
    for layer_idx in (1, 0):
        weight_rows = fetch_again(low_tiles[layer_idx])
        grad_state, frame_grads[layer_idx], bias_grads[layer_idx], tile_grads[layer_idx] = (
            backward_block(
                grad_state,
                kept[layer_idx],
                frame_mod[layer_idx],
                weight_rows,
                layer_idx == 1,
                masks[layer_idx],
                col_start,
                col_width,
            )
        )
    input_grad = grad_state.reshape(frames * PATCHES, col_width)
    grad_clip_mod = jnp.einsum(
        "fc,lfke->lcke", pick, jnp.stack(frame_grads), precision=HIGHEST_PREC
    )
    grad_clip_mod, grad_lin = (
        lax.psum(grad_clip_mod.astype(jnp.bfloat16), "wide").astype(jnp.float32),
        lax.psum(jnp.stack(bias_grads).astype(jnp.bfloat16), "wide").astype(jnp.float32),
    )
    grad_ada = jnp.einsum("cd,lcke->ldke", cond_rows, grad_clip_mod, precision=HIGHEST_PREC)
    grad_bias = jnp.concatenate([grad_lin, jnp.sum(grad_clip_mod, axis=1)], axis=1)
    grad_tiles = [
        jnp.stack([tile_grads[0][slot_index], tile_grads[1][slot_index]]) for slot_index in range(4)
    ]
    gradients = (grad_tiles[0], grad_tiles[1], grad_tiles[2], grad_tiles[3], grad_ada, grad_bias)
    masters = (qkv_weight, out_weight, up_weight, down_weight, ada_weight, bias_weight)
    firsts = (qkv_first, out_first, up_first, down_first, ada_first, bias_first)
    seconds = (qkv_second, out_second, up_second, down_second, ada_second, bias_second)
    shares = (1.0, 1.0, 1.0, 1.0, 1.0, 1.0 / wide_count)
    local_sq = jnp.zeros((), jnp.float32)
    for gradient, share_of in zip(gradients, shares):
        local_sq = local_sq + jnp.sum(gradient * gradient) * share_of
    grad_norm = jnp.sqrt(lax.psum(local_sq, ("wide", "narrow")))
    factor = jnp.minimum(1.0, CLIP_LIMIT / grad_norm)
    first_fix = 1.0 - BETA_ONE**STEP
    second_fix = 1.0 - BETA_TWO**STEP
    updates = []
    states = []
    norm_terms = []
    for master, first_in, second_in, gradient, share_of in zip(
        masters, firsts, seconds, gradients, shares
    ):
        clipped = gradient * factor
        moment = BETA_ONE * first_in + (1.0 - BETA_ONE) * clipped
        square = BETA_TWO * second_in + (1.0 - BETA_TWO) * clipped * clipped
        update = (
            moment / first_fix / (jnp.sqrt(square / second_fix) + ADAM_EPS) + WEIGHT_DECAY * master
        )
        updates.append(update)
        states.append((moment, square))
        norm_terms.append(
            jnp.stack(
                [
                    jnp.sum((master * master).reshape(2, -1), axis=1),
                    jnp.sum((update * update).reshape(2, -1), axis=1),
                ],
                axis=1,
            )
            * share_of
        )
    trust_norms = jnp.sqrt(lax.psum(jnp.stack(norm_terms, axis=1), ("wide", "narrow")))
    trust_ratio = trust_norms[:, :, 0] / trust_norms[:, :, 1]
    results = []
    for position in range(6):
        master = masters[position]
        ratio_here = trust_ratio[:, position].reshape((2,) + (1,) * (master.ndim - 1))
        results.append(
            (
                master - LEARN_RATE * ratio_here * updates[position],
                states[position][0],
                states[position][1],
            )
        )
    return (
        block_output,
        input_grad,
        results[0][0],
        results[0][1],
        results[0][2],
        results[1][0],
        results[1][1],
        results[1][2],
        results[2][0],
        results[2][1],
        results[2][2],
        results[3][0],
        results[3][1],
        results[3][2],
        results[4][0],
        results[4][1],
        results[4][2],
        results[5][0],
        results[5][1],
        results[5][2],
        trust_norms,
        grad_norm.reshape(1),
    )


def solution(mesh):
    return jax.shard_map(
        on_device,
        mesh=mesh,
        in_specs=(
            P("wide", "narrow"),
            P(),
            P(),
            P("wide", "narrow"),
            P(None, "wide", None, "narrow"),
            P(None, "wide", None, "narrow"),
            P(None, "wide", None, "narrow"),
            P(None, "wide", "narrow"),
            P(None, "wide", "narrow"),
            P(None, "wide", "narrow"),
            P(None, "wide", None, "narrow"),
            P(None, "wide", None, "narrow"),
            P(None, "wide", None, "narrow"),
            P(None, "wide", None, "narrow"),
            P(None, "wide", None, "narrow"),
            P(None, "wide", None, "narrow"),
            P(None, "wide", None, "narrow"),
            P(None, "wide", None, "narrow"),
            P(None, "wide", None, "narrow"),
            P(None, None, "narrow"),
            P(None, None, "narrow"),
            P(None, None, "narrow"),
        ),
        out_specs=(
            P("wide", "narrow"),
            P("wide", "narrow"),
            P(None, "wide", None, "narrow"),
            P(None, "wide", None, "narrow"),
            P(None, "wide", None, "narrow"),
            P(None, "wide", "narrow"),
            P(None, "wide", "narrow"),
            P(None, "wide", "narrow"),
            P(None, "wide", None, "narrow"),
            P(None, "wide", None, "narrow"),
            P(None, "wide", None, "narrow"),
            P(None, "wide", None, "narrow"),
            P(None, "wide", None, "narrow"),
            P(None, "wide", None, "narrow"),
            P(None, "wide", None, "narrow"),
            P(None, "wide", None, "narrow"),
            P(None, "wide", None, "narrow"),
            P(None, None, "narrow"),
            P(None, None, "narrow"),
            P(None, None, "narrow"),
            P(),
            P(),
        ),
        check_vma=False,
    )
```

profile of v0, /device:TPU:0, one launch (start us, length us, event | category | flops | bytes accessed | tf_op | source)
XLA Modules:
  0.0 2668.4 jit_solution(11074682505051096973)
XLA Ops:
  19.9 36.6 %all-gather.1 = bf16[1,1152,288]{2,1,0:T(8,128)(2,1)} all-gather(bf16[1,144,288]{2,1,0:T(8,128)(2,1)S(1)} %get-tuple-element.214), channel_id=3, replica_groups=mesh['wide'=8,'narrow'=4] {'wide'}, dimensions={1}, use_global_device_ids=true | all-gather | bytes 746496 | tf_op jit(solution)/shard_map/all_gather | solution.py:44
  56.5 125.5 %all-reduce.7.cloned.1.call-done = f32[2,4,6,1152]{3,1,2,0:T(4,128)} async-done(((f32[2,4,6,1152]{3,1,2,0:T(4,128)}), f32[2,4,6,1152]{3,1,2,0:T(4,128)}) %all-reduce.7.cloned.1.call-update) | async-done | bytes 221200 | tf_op jit(solution)/shard_map/psum | solution.py:398
  224.6 42.5 %reduce-scatter.17.cloned.1.call-done = bf16[8,256,288]{1,2,0:T(8,128)(2,1)} async-done(((bf16[8,256,1152]{1,2,0:T(8,128)(2,1)}), bf16[8,256,288]{1,2,0:T(8,128)(2,1)}) %reduce-scatter.17.cloned.1.call-update) | async-done | bytes 1179664 | tf_op jit(solution)/shard_map/reduce_scatter | solution.py:28
  271.8 63.1 %all-gather.41.cloned.1.call-done = bf16[1,1152,4,288]{3,2,0,1:T(4,128)(2,1)} async-done(((bf16[1,144,4,288]{3,2,0,1:T(4,128)(2,1)}), bf16[1,1152,4,288]{3,2,0,1:T(4,128)(2,1)}) %all-gather.41.cloned.1.call-update) | async-done | bytes 2654224 | tf_op jit(solution)/shard_map/all_gather | solution.py:45
  342.2 59.1 %all-gather.43.cloned.1.call-done = bf16[1,1152,4,288]{3,2,0,1:T(4,128)(2,1)} async-done(((bf16[1,144,4,288]{3,2,0,1:T(4,128)(2,1)}), bf16[1,1152,4,288]{3,2,0,1:T(4,128)(2,1)}) %all-gather.43.cloned.1.call-update) | async-done | bytes 2654224 | tf_op jit(solution)/shard_map/all_gather | solution.py:46
  408.5 31.0 %all-gather.25.cloned.1.call-done = bf16[8,256,1152]{1,2,0:T(8,128)(2,1)} async-done(((bf16[8,256,288]{1,2,0:T(8,128)(2,1)}), bf16[8,256,1152]{1,2,0:T(8,128)(2,1)}) %all-gather.25.cloned.1.call-update) | async-done | bytes 4718608 | tf_op jit(solution)/shard_map/all_gather | solution.py:24
  468.6 46.3 %reduce-scatter.19.cloned.1.call-done = bf16[8,256,288]{1,2,0:T(8,128)(2,1)} async-done(((bf16[8,256,1152]{1,2,0:T(8,128)(2,1)}), bf16[8,256,288]{1,2,0:T(8,128)(2,1)}) %reduce-scatter.19.cloned.1.call-update) | async-done | bytes 1179664 | tf_op jit(solution)/shard_map/reduce_scatter | solution.py:28
  519.9 35.3 %all-gather.27.cloned.1.call-done = bf16[8,256,1152]{1,2,0:T(8,128)(2,1)} async-done(((bf16[8,256,288]{1,2,0:T(8,128)(2,1)}), bf16[8,256,1152]{1,2,0:T(8,128)(2,1)}) %all-gather.27.cloned.1.call-update) | async-done | bytes 4718608 | tf_op jit(solution)/shard_map/all_gather | solution.py:24
  560.7 52.2 %all-gather.45.cloned.1.call-done = bf16[1,1152,3,288]{3,1,2,0:T(8,128)(2,1)} async-done(((bf16[1,144,3,288]{3,1,2,0:T(8,128)(2,1)}), bf16[1,1152,3,288]{3,1,2,0:T(8,128)(2,1)}) %all-gather.45.cloned.1.call-update) | async-done | bytes 1990672 | tf_op jit(solution)/shard_map/all_gather | solution.py:43
  635.7 102.0 %all-to-all-done = bf16[3,8,256,288]{3,1,0,2:T(8,128)(2,1)} async-done(((bf16[3,8,256,288]{3,1,0,2:T(8,128)(2,1)}), bf16[3,8,256,288]{3,1,0,2:T(8,128)(2,1)}, u32[]{:S(2)}, u32[]{:S(2)}) %all-to-all-start) | async-done | bytes 3538976 | tf_op jit(solution)/shard_map/all_to_all | solution.py:34
  743.2 12.3 reshape.348
  795.0 61.2 %all-gather.5 = bf16[1,1152,288]{2,1,0:T(8,128)(2,1)} all-gather(bf16[1,144,288]{2,1,0:T(8,128)(2,1)} %get-tuple-element.213), channel_id=7, replica_groups=mesh['wide'=8,'narrow'=4] {'wide'}, dimensions={1}, use_global_device_ids=true | all-gather | bytes 746496 | tf_op jit(solution)/shard_map/all_gather | solution.py:44
  866.7 44.1 %reduce-scatter.21.cloned.1.call-done = bf16[8,256,288]{1,2,0:T(8,128)(2,1)} async-done(((bf16[8,256,1152]{1,2,0:T(8,128)(2,1)}), bf16[8,256,288]{1,2,0:T(8,128)(2,1)}) %reduce-scatter.21.cloned.1.call-update) | async-done | bytes 1179664 | tf_op jit(solution)/shard_map/reduce_scatter | solution.py:28
  916.2 62.2 %all-gather.47.cloned.1.call-done = bf16[1,1152,4,288]{3,2,0,1:T(4,128)(2,1)} async-done(((bf16[1,144,4,288]{3,2,0,1:T(4,128)(2,1)}), bf16[1,1152,4,288]{3,2,0,1:T(4,128)(2,1)}) %all-gather.47.cloned.1.call-update) | async-done | bytes 2654224 | tf_op jit(solution)/shard_map/all_gather | solution.py:45
  985.7 59.1 %all-gather.49.cloned.1.call-done = bf16[1,1152,4,288]{3,2,0,1:T(4,128)(2,1)} async-done(((bf16[1,144,4,288]{3,2,0,1:T(4,128)(2,1)}), bf16[1,1152,4,288]{3,2,0,1:T(4,128)(2,1)}) %all-gather.49.cloned.1.call-update) | async-done | bytes 2654224 | tf_op jit(solution)/shard_map/all_gather | solution.py:46
  1052.1 30.8 %all-gather.29.cloned.1.call-done = bf16[8,256,1152]{1,2,0:T(8,128)(2,1)} async-done(((bf16[8,256,288]{1,2,0:T(8,128)(2,1)}), bf16[8,256,1152]{1,2,0:T(8,128)(2,1)}) %all-gather.29.cloned.1.call-update) | async-done | bytes 4718608 | tf_op jit(solution)/shard_map/all_gather | solution.py:24
  1112.2 46.2 %reduce-scatter.23.cloned.1.call-done = bf16[8,256,288]{1,2,0:T(8,128)(2,1)} async-done(((bf16[8,256,1152]{1,2,0:T(8,128)(2,1)}), bf16[8,256,288]{1,2,0:T(8,128)(2,1)}) %reduce-scatter.23.cloned.1.call-update) | async-done | bytes 1179664 | tf_op jit(solution)/shard_map/reduce_scatter | solution.py:28
  1164.1 37.3 %all-gather.31.cloned.1.call-done = bf16[8,256,1152]{1,2,0:T(8,128)(2,1)} async-done(((bf16[8,256,288]{1,2,0:T(8,128)(2,1)}), bf16[8,256,1152]{1,2,0:T(8,128)(2,1)}) %all-gather.31.cloned.1.call-update) | async-done | bytes 4718608 | tf_op jit(solution)/shard_map/all_gather | solution.py:24
  1201.4 17.6 fusion.208
  1239.0 38.1 %reduce-scatter.25.cloned.1.call-done = bf16[8,256,288]{1,2,0:T(8,128)(2,1)} async-done(((bf16[8,256,1152]{1,2,0:T(8,128)(2,1)}), bf16[8,256,288]{1,2,0:T(8,128)(2,1)}) %reduce-scatter.25.cloned.1.call-update) | async-done | bytes 1179664 | tf_op jit(solution)/shard_map/reduce_scatter | solution.py:170
  1281.3 11.3 all-reduce.3
  1297.6 38.0 %all-gather.33.cloned.1.call-done = bf16[8,256,1152]{1,2,0:T(8,128)(2,1)} async-done(((bf16[8,256,288]{1,2,0:T(8,128)(2,1)}), bf16[8,256,1152]{1,2,0:T(8,128)(2,1)}) %all-gather.33.cloned.1.call-update) | async-done | bytes 4718608 | tf_op jit(solution)/shard_map/all_gather | solution.py:24
  1341.3 42.9 %all_to_all.63 = bf16[1,8,256,288]{3,1,0,2:T(8,128)(2,1)S(1)} all-to-all(bf16[1,8,256,288]{3,1,0,2:T(8,128)(2,1)S(1)} %copy.294), channel_id=1, replica_groups=mesh['wide'=8,'narrow'=4] {'wide'}, dimensions={2} | all-to-all | bytes 2359296 | tf_op jit(solution)/shard_map/all_to_all | solution.py:34
  1403.3 14.9 maximum_bitcast_fusion
  1431.8 107.8 %all_to_all.64 = bf16[3,64,32,288]{3,2,0,1:T(8,128)(2,1)S(1)} all-to-all(bf16[3,64,32,288]{3,2,0,1:T(8,128)(2,1)S(1)} %copy.302), channel_id=1, replica_groups=mesh['wide'=8,'narrow'=4] {'wide'}, dimensions={1} | all-to-all | bytes 7077888 | tf_op jit(solution)/shard_map/all_to_all | solution.py:38
  1561.9 36.2 %reduce-scatter.27.cloned.1.call-done = bf16[8,256,288]{1,2,0:T(8,128)(2,1)} async-done(((bf16[8,256,1152]{1,2,0:T(8,128)(2,1)}), bf16[8,256,288]{1,2,0:T(8,128)(2,1)}) %reduce-scatter.27.cloned.1.call-update) | async-done | bytes 1179664 | tf_op jit(solution)/shard_map/reduce_scatter | solution.py:170
  1602.2 11.3 all-reduce.2
  1619.2 38.0 %all-gather.35.cloned.1.call-done = bf16[8,256,1152]{1,2,0:T(8,128)(2,1)} async-done(((bf16[8,256,288]{1,2,0:T(8,128)(2,1)}), bf16[8,256,1152]{1,2,0:T(8,128)(2,1)}) %all-gather.35.cloned.1.call-update) | async-done | bytes 4718608 | tf_op jit(solution)/shard_map/all_gather | solution.py:24
  1657.3 17.8 fusion.209
  1695.0 38.1 %reduce-scatter.29.cloned.1.call-done = bf16[8,256,288]{1,2,0:T(8,128)(2,1)} async-done(((bf16[8,256,1152]{1,2,0:T(8,128)(2,1)}), bf16[8,256,288]{1,2,0:T(8,128)(2,1)}) %reduce-scatter.29.cloned.1.call-update) | async-done | bytes 1179664 | tf_op jit(solution)/shard_map/reduce_scatter | solution.py:170
  1737.2 11.3 all-reduce.1
  1754.4 13.4 bitcast_convert_fusion.6
  1768.4 13.3 bitcast_convert_fusion.7
  1782.6 11.9 bitcast_convert_fusion.8
  1795.3 11.9 bitcast_convert_fusion.9
  1820.7 11.8 bitcast_convert_fusion.11
  1909.5 48.1 %reduce-scatter.45.cloned.1.call-done = bf16[144,4,288]{2,0,1:T(8,128)(2,1)} async-done(((bf16[1152,4,288]{2,0,1:T(8,128)(2,1)}), bf16[144,4,288]{2,0,1:T(8,128)(2,1)}) %reduce-scatter.45.cloned.1.call-update) | async-done | bytes 331792 | tf_op jit(solution)/shard_map/reduce_scatter | solution.py:323
  1959.9 80.4 %reduce-scatter.43.cloned.1.call-done = bf16[144,4,288]{2,0,1:T(8,128)(2,1)} async-done(((bf16[1152,4,288]{2,0,1:T(8,128)(2,1)}), bf16[144,4,288]{2,0,1:T(8,128)(2,1)}) %reduce-scatter.43.cloned.1.call-update) | async-done | bytes 331792 | tf_op jit(solution)/shard_map/reduce_scatter | solution.py:320
  2040.3 82.5 %reduce-scatter.41.cloned.1.call-done = bf16[144,4,288]{2,0,1:T(8,128)(2,1)} async-done(((bf16[1152,4,288]{2,0,1:T(8,128)(2,1)}), bf16[144,4,288]{2,0,1:T(8,128)(2,1)}) %reduce-scatter.41.cloned.1.call-update) | async-done | bytes 331792 | tf_op jit(solution)/shard_map/reduce_scatter | solution.py:320
  2132.3 55.4 %reduce-scatter.39.cloned.1.call-done = bf16[144,288]{1,0:T(8,128)(2,1)} async-done(((bf16[1152,288]{1,0:T(8,128)(2,1)}), bf16[144,288]{1,0:T(8,128)(2,1)}) %reduce-scatter.39.cloned.1.call-update) | async-done | bytes 82960 | tf_op jit(solution)/shard_map/reduce_scatter | solution.py:317
  2187.8 64.6 %reduce-scatter.37.cloned.1.call-done = bf16[144,288]{1,0:T(8,128)(2,1)} async-done(((bf16[1152,288]{1,0:T(8,128)(2,1)}), bf16[144,288]{1,0:T(8,128)(2,1)}) %reduce-scatter.37.cloned.1.call-update) | async-done | bytes 82960 | tf_op jit(solution)/shard_map/reduce_scatter | solution.py:317
  2254.1 72.4 %reduce-scatter.35.cloned.1.call-done = bf16[144,3,288]{2,0,1:T(8,128)(2,1)} async-done(((bf16[1152,3,288]{2,0,1:T(8,128)(2,1)}), bf16[144,3,288]{2,0,1:T(8,128)(2,1)}) %reduce-scatter.35.cloned.1.call-update) | async-done | bytes 248848 | tf_op jit(solution)/shard_map/reduce_scatter | solution.py:314
  2326.5 73.7 %reduce-scatter.33.cloned.1.call-done = bf16[144,3,288]{2,0,1:T(8,128)(2,1)} async-done(((bf16[1152,3,288]{2,0,1:T(8,128)(2,1)}), bf16[144,3,288]{2,0,1:T(8,128)(2,1)}) %reduce-scatter.33.cloned.1.call-update) | async-done | bytes 248848 | tf_op jit(solution)/shard_map/reduce_scatter | solution.py:314
  2404.8 44.8 %reduce-scatter.31.cloned.1.call-done = bf16[8,256,288]{1,2,0:T(8,128)(2,1)} async-done(((bf16[8,256,1152]{1,2,0:T(8,128)(2,1)}), bf16[8,256,288]{1,2,0:T(8,128)(2,1)}) %reduce-scatter.31.cloned.1.call-update) | async-done | bytes 1179664 | tf_op jit(solution)/shard_map/reduce_scatter | solution.py:170
  2453.6 11.3 all-reduce
  2472.7 38.3 %all-reduce.4 = (bf16[2,4,6,288]{3,1,2,0:T(4,128)(2,1)S(1)}, bf16[2,8,288]{2,1,0:T(8,128)(2,1)S(1)}) all-reduce(bf16[2,4,6,288]{3,1,2,0:T(4,128)(2,1)S(1)} %fusion.143, bf16[2,8,288]{2,1,0:T(8,128)(2,1)} %pad_maximum_fusion.6), channel_id=1, replica_groups=mesh['wide'=8,'narrow'=4] {'wide'}, use_global_device_ids=true, to_apply=%region_64.65 | all-reduce | flops 18432 | bytes 73728 | tf_op jit(solution)/shard_map/psum | solution.py:459
  2518.9 36.8 %psum.102 = f32[]{:T(128)} all-reduce(f32[]{:T(128)S(6)} %add.496), channel_id=1, replica_groups=mesh['wide'=8,'narrow'=4] {'wide','narrow'}, use_global_device_ids=true, to_apply=%region_77.78 | all-reduce | flops 1 | bytes 8 | tf_op jit(solution)/shard_map/psum | solution.py:475
  2598.4 42.3 %psum.103 = f32[2,6,2]{1,2,0:T(2,128)S(1)} all-reduce(f32[2,6,2]{1,2,0:T(2,128)S(1)} %copy-done.123), channel_id=1, replica_groups=mesh['wide'=8,'narrow'=4] {'wide','narrow'}, use_global_device_ids=true, to_apply=%region_89.90 | all-reduce | flops 24 | bytes 192 | tf_op jit(solution)/shard_map/psum | solution.py:503
  (582 shorter events, 561.6 us)
Async XLA Ops:
  8.0 174.0 %all-reduce.7.cloned.1.call-start = ((), (), s32[]{:S(2)}) async-start(), calls=%async_computation.20 | async-start | bytes 442368 | tf_op jit(solution)/shard_map/psum | solution.py:398
  13.4 171.4 %all-gather.23.cloned.1.call-start = ((), (), s32[]{:S(2)}) async-start(), calls=%async_computation.21 | async-start | bytes 5898240 | tf_op jit(solution)/shard_map/all_gather | solution.py:24
  14.6 175.3 %all-gather.39.cloned.1.call-start = ((), (), s32[]{:S(2)}) async-start(), calls=%async_computation.45 | async-start | bytes 2985984 | tf_op jit(solution)/shard_map/all_gather | solution.py:43
  17.0 250.1 %reduce-scatter.17.cloned.1.call-start = ((), (), s32[]{:S(2)}) async-start(), calls=%async_computation.22 | async-start | bytes 5898240 | tf_op jit(solution)/shard_map/reduce_scatter | solution.py:28
  17.2 166.9 %copy-start.129 = (s32[8]{0:T(128)}, s32[8]{0:T(128)S(1)}, u32[]{:S(2)}) copy-start(s32[8]{0:T(128)S(1)} %and_select_fusion) | copy-start | bytes 100
  18.6 1139.8 %copy-start.76 = (f32[288]{0:T(512)}, f32[288]{0:T(512)S(1)}, u32[]{:S(2)}) copy-start(f32[288]{0:T(512)S(1)} %get-tuple-element.220) | copy-start | bytes 3460
  218.3 116.6 %all-gather.41.cloned.1.call-start = ((), (), s32[]{:S(2)}) async-start(), calls=%async_computation.46 | async-start | bytes 3981312 | tf_op jit(solution)/shard_map/all_gather | solution.py:45
  221.0 180.3 %all-gather.43.cloned.1.call-start = ((), (), s32[]{:S(2)}) async-start(), calls=%async_computation.47 | async-start | bytes 3981312 | tf_op jit(solution)/shard_map/all_gather | solution.py:46
  223.7 215.8 %all-gather.25.cloned.1.call-start = ((), (), s32[]{:S(2)}) async-start(), calls=%async_computation.23 | async-start | bytes 5898240 | tf_op jit(solution)/shard_map/all_gather | solution.py:24
  269.8 245.1 %reduce-scatter.19.cloned.1.call-start = ((), (), s32[]{:S(2)}) async-start(), calls=%async_computation.24 | async-start | bytes 5898240 | tf_op jit(solution)/shard_map/reduce_scatter | solution.py:28
  271.8 181.7 %copy-start.125 = (f32[1,4,288]{2,1,0:T(4,128)}, f32[1,4,288]{2,1,0:T(4,128)S(1)}, u32[]{:S(2)}) copy-start(f32[1,4,288]{2,1,0:T(4,128)S(1)} %copy.478) | copy-start | bytes 13828
  467.0 47.9 %copy-start.6 = (bf16[8,256,288]{1,2,0:T(8,128)(2,1)S(1)}, bf16[8,256,288]{1,2,0:T(8,128)(2,1)}, u32[]{:S(2)}) copy-start(bf16[8,256,288]{1,2,0:T(8,128)(2,1)} %reduce-scatter.17.cloned.1.call-done) | copy-start | bytes 3538948
  467.0 88.1 %all-gather.27.cloned.1.call-start = ((), (), s32[]{:S(2)}) async-start(), calls=%async_computation.25 | async-start | bytes 5898240 | tf_op jit(solution)/shard_map/all_gather | solution.py:24
  517.7 95.2 %all-gather.45.cloned.1.call-start = ((), (), s32[]{:S(2)}) async-start(), calls=%async_computation.48 | async-start | bytes 2985984 | tf_op jit(solution)/shard_map/all_gather | solution.py:43
  629.9 107.9 %all-to-all-start = ((bf16[3,8,256,288]{3,1,0,2:T(8,128)(2,1)}), bf16[3,8,256,288]{3,1,0,2:T(8,128)(2,1)}, u32[]{:S(2)}, u32[]{:S(2)}) async-start(bf16[3,8,256,288]{3,1,0,2:T(8,128)(2,1)} %copy.276), calls=%async_computation.2 | async-start | bytes 9437184 | tf_op jit(solution)/shard_map/all_to_all | solution.py:34
  790.6 65.6 %all-to-all-start.1 = ((bf16[1,64,32,288]{3,2,0,1:T(8,128)(2,1)}), bf16[1,64,32,288]{3,2,0,1:T(8,128)(2,1)}, u32[]{:S(2)}, u32[]{:S(2)}) async-start(bf16[1,64,32,288]{3,2,0,1:T(8,128)(2,1)} %bitcast.517), calls=%async_computation.3 | async-start | bytes 3145728 | tf_op jit(solution)/shard_map/all_to_all | solution.py:38
  794.9 115.9 %reduce-scatter.21.cloned.1.call-start = ((), (), s32[]{:S(2)}) async-start(), calls=%async_computation.26 | async-start | bytes 5898240 | tf_op jit(solution)/shard_map/reduce_scatter | solution.py:28
  863.9 114.5 %all-gather.47.cloned.1.call-start = ((), (), s32[]{:S(2)}) async-start(), calls=%async_computation.49 | async-start | bytes 3981312 | tf_op jit(solution)/shard_map/all_gather | solution.py:45
  864.5 180.3 %all-gather.49.cloned.1.call-start = ((), (), s32[]{:S(2)}) async-start(), calls=%async_computation.50 | async-start | bytes 3981312 | tf_op jit(solution)/shard_map/all_gather | solution.py:46
  865.3 217.6 %all-gather.29.cloned.1.call-start = ((), (), s32[]{:S(2)}) async-start(), calls=%async_computation.27 | async-start | bytes 5898240 | tf_op jit(solution)/shard_map/all_gather | solution.py:24
  914.9 243.5 %reduce-scatter.23.cloned.1.call-start = ((), (), s32[]{:S(2)}) async-start(), calls=%async_computation.28 | async-start | bytes 5898240 | tf_op jit(solution)/shard_map/reduce_scatter | solution.py:28
  1110.5 90.9 %all-gather.31.cloned.1.call-start = ((), (), s32[]{:S(2)}) async-start(), calls=%async_computation.29 | async-start | bytes 5898240 | tf_op jit(solution)/shard_map/all_gather | solution.py:24
  1164.0 57.3 %copy-start.50 = (bf16[1,1152,4,288]{1,3,2,0:T(8,128)(2,1)S(1)}, bf16[1,1152,4,288]{1,3,2,0:T(8,128)(2,1)}, u32[]{:S(2)}) copy-start(bf16[1,1152,4,288]{1,3,2,0:T(8,128)(2,1)} %copy.288) | copy-start | bytes 7962628
  1164.0 113.1 %reduce-scatter.25.cloned.1.call-start = ((), (), s32[]{:S(2)}) async-start(), calls=%async_computation.30 | async-start | bytes 5898240 | tf_op jit(solution)/shard_map/reduce_scatter | solution.py:170
  1229.3 106.4 %all-gather.33.cloned.1.call-start = ((), (), s32[]{:S(2)}) async-start(), calls=%async_computation.31 | async-start | bytes 5898240 | tf_op jit(solution)/shard_map/all_gather | solution.py:24
  1239.0 54.3 %copy-start.13 = (f32[2048,288]{0,1:T(8,128)S(1)}, f32[2048,288]{0,1:T(8,128)}, u32[]{:S(2)}) copy-start(f32[2048,288]{0,1:T(8,128)} %param.25) | copy-start | bytes 7077892
  1297.6 300.5 %reduce-scatter.27.cloned.1.call-start = ((), (), s32[]{:S(2)}) async-start(), calls=%async_computation.32 | async-start | bytes 5898240 | tf_op jit(solution)/shard_map/reduce_scatter | solution.py:170
  1552.2 105.1 %all-gather.35.cloned.1.call-start = ((), (), s32[]{:S(2)}) async-start(), calls=%async_computation.33 | async-start | bytes 5898240 | tf_op jit(solution)/shard_map/all_gather | solution.py:24
  1561.9 53.0 %copy-start.15 = (f32[8,256,288]{1,2,0:T(8,128)S(1)}, f32[8,256,288]{1,2,0:T(8,128)}, u32[]{:S(2)}) copy-start(f32[8,256,288]{1,2,0:T(8,128)} %get-tuple-element.177) | copy-start | bytes 7077892
  1619.2 58.1 %copy-start.47 = (bf16[1,1152,4,288]{1,3,2,0:T(8,128)(2,1)S(1)}, bf16[1,1152,4,288]{1,3,2,0:T(8,128)(2,1)}, u32[]{:S(2)}) copy-start(bf16[1,1152,4,288]{1,3,2,0:T(8,128)(2,1)} %copy.270) | copy-start | bytes 7962628
  1619.2 113.9 %reduce-scatter.29.cloned.1.call-start = ((), (), s32[]{:S(2)}) async-start(), calls=%async_computation.34 | async-start | bytes 5898240 | tf_op jit(solution)/shard_map/reduce_scatter | solution.py:170
  1685.3 129.4 %all-gather.37.cloned.1.call-start = ((), (), s32[]{:S(2)}) async-start(), calls=%async_computation.35 | async-start | bytes 5898240 | tf_op jit(solution)/shard_map/all_gather | solution.py:24
  1695.0 55.0 %copy-start.17 = (f32[8,256,288]{1,2,0:T(8,128)S(1)}, f32[8,256,288]{1,2,0:T(8,128)}, u32[]{:S(2)}) copy-start(f32[8,256,288]{1,2,0:T(8,128)} %get-tuple-element.171) | copy-start | bytes 7077892
  1754.1 155.4 %reduce-scatter.47.cloned.1.call-start = ((), (), s32[]{:S(2)}) async-start(), calls=%async_computation.44 | async-start | bytes 3981312 | tf_op jit(solution)/shard_map/reduce_scatter | solution.py:323
  1767.8 189.9 %reduce-scatter.45.cloned.1.call-start = ((), (), s32[]{:S(2)}) async-start(), calls=%async_computation.43 | async-start | bytes 3981312 | tf_op jit(solution)/shard_map/reduce_scatter | solution.py:323
  1781.8 258.4 %reduce-scatter.43.cloned.1.call-start = ((), (), s32[]{:S(2)}) async-start(), calls=%async_computation.42 | async-start | bytes 3981312 | tf_op jit(solution)/shard_map/reduce_scatter | solution.py:320
  1794.5 328.2 %reduce-scatter.41.cloned.1.call-start = ((), (), s32[]{:S(2)}) async-start(), calls=%async_computation.41 | async-start | bytes 3981312 | tf_op jit(solution)/shard_map/reduce_scatter | solution.py:320
  1807.3 380.5 %reduce-scatter.39.cloned.1.call-start = ((), (), s32[]{:S(2)}) async-start(), calls=%async_computation.40 | async-start | bytes 995328 | tf_op jit(solution)/shard_map/reduce_scatter | solution.py:317
  1814.6 437.8 %reduce-scatter.37.cloned.1.call-start = ((), (), s32[]{:S(2)}) async-start(), calls=%async_computation.39 | async-start | bytes 995328 | tf_op jit(solution)/shard_map/reduce_scatter | solution.py:317
  1820.6 505.9 %reduce-scatter.35.cloned.1.call-start = ((), (), s32[]{:S(2)}) async-start(), calls=%async_computation.38 | async-start | bytes 2985984 | tf_op jit(solution)/shard_map/reduce_scatter | solution.py:314
  1832.6 567.6 %reduce-scatter.33.cloned.1.call-start = ((), (), s32[]{:S(2)}) async-start(), calls=%async_computation.37 | async-start | bytes 2985984 | tf_op jit(solution)/shard_map/reduce_scatter | solution.py:314
  1864.3 585.3 %reduce-scatter.31.cloned.1.call-start = ((), (), s32[]{:S(2)}) async-start(), calls=%async_computation.36 | async-start | bytes 5898240 | tf_op jit(solution)/shard_map/reduce_scatter | solution.py:170
  2128.8 338.9 %copy-start.7 = (bf16[8,256,288]{1,2,0:T(8,128)(2,1)S(1)}, bf16[8,256,288]{1,2,0:T(8,128)(2,1)}, u32[]{:S(2)}) copy-start(bf16[8,256,288]{1,2,0:T(8,128)(2,1)} %reduce-scatter.17.cloned.1.call-done) | copy-start | bytes 3538948
  2128.8 338.9 %copy-start.24 = (f32[8,256,288]{1,2,0:T(8,128)S(1)}, f32[8,256,288]{1,2,0:T(8,128)}, u32[]{:S(2)}) copy-start(f32[8,256,288]{1,2,0:T(8,128)} %get-tuple-element.174) | copy-start | bytes 7077892
  2128.8 338.9 %copy-start.77 = (f32[288]{0:T(512)S(1)}, f32[288]{0:T(512)}, u32[]{:S(2)}) copy-start(f32[288]{0:T(512)} %copy-done.76) | copy-start | bytes 3460
  2471.4 45.8 %copy-start.26 = (f32[8,36,8,256]{3,2,1,0:T(8,128)S(1)}, f32[8,36,8,256]{3,2,1,0:T(8,128)}, u32[]{:S(2)}) copy-start(f32[8,36,8,256]{3,2,1,0:T(8,128)} %get-tuple-element.185) | copy-start | bytes 7077892
  2515.2 42.8 %copy-start.45 = (f32[2,144,288]{2,1,0:T(8,128)S(1)}, f32[2,144,288]{2,1,0:T(8,128)}, u32[]{:S(2)}) copy-start(f32[2,144,288]{2,1,0:T(8,128)} %param.29) | copy-start | bytes 995332
  2560.4 92.3 %copy-start.53 = (f32[2,144,288]{2,1,0:T(8,128)}, f32[2,144,288]{2,1,0:T(8,128)S(1)}, u32[]{:S(2)}) copy-start(f32[2,144,288]{2,1,0:T(8,128)S(1)} %get-tuple-element.165) | copy-start | bytes 995332
  (135 other events, 826.8 us)
Sparse Core Ops, SparseCore 0:
  15.0 166.9 all-reduce.6
Sparse Core Ops, SparseCore 1:
  16.0 41.7 all-gather.22
  60.4 55.1 all-gather.38
  218.4 48.7 reduce-scatter.16
  270.1 64.7 all-gather.40
  337.9 63.3 all-gather.42
  403.5 35.9 all-gather.24
  467.1 47.7 reduce-scatter.18
  517.8 37.3 all-gather.26
  557.8 55.0 all-gather.44
  864.0 46.7 reduce-scatter.20
  913.7 64.7 all-gather.46
  981.4 63.3 all-gather.48
  1046.9 35.9 all-gather.28
  1110.6 47.7 reduce-scatter.22
  1164.1 37.3 all-gather.30
  1229.4 47.7 reduce-scatter.24
  1297.7 37.9 all-gather.32
  1552.3 45.8 reduce-scatter.26
  1619.3 37.9 all-gather.34
  1685.3 47.7 reduce-scatter.28
  1754.2 38.0 all-gather.36
  1796.2 79.0 reduce-scatter.46
  1879.2 78.4 reduce-scatter.44
  1961.8 78.4 reduce-scatter.42
  2044.2 78.5 reduce-scatter.40
  2127.1 60.6 reduce-scatter.38
  2192.2 60.2 reduce-scatter.36
  2257.0 69.5 reduce-scatter.34
  2330.6 69.5 reduce-scatter.32
  2402.9 46.6 reduce-scatter.30
where the time goes:
time: 2680 us; the launch traced here: 2670 us
  waiting for transfers between devices  1550 us (58%)
  blocking collectives  411 us (15%)
  matrix products  276 us (10%)
  local copies, waits for them, and re-layouts  205 us (8%)
  other arithmetic  192 us (7%)
    all_gather x8, waiting for transfers between devices, whole_rows(): return lax.all_gather(fragment, 'narrow', axis=2, tiled=True)  210 us
    reduce_scatter x4, waiting for transfers between devices, sum_columns(): lax.psum_scatter(partial_sum.astype(jnp.bfloat16), 'narrow', scatter_dime...  179 us
    reduce_scatter x2, waiting for transfers between devices, backward_block(): lax.psum_scatter(grad_up.astype(jnp.bfloat16), 'wide', scatter_dimension=...  163 us
    reduce_scatter x4, waiting for transfers between devices, norm_backward(): lax.psum_scatter(partial_sum.astype(jnp.bfloat16), 'narrow', scatter_dime...  157 us
    reduce_scatter x2, waiting for transfers between devices, backward_block(): lax.psum_scatter(grad_qkv_weight.astype(jnp.bfloat16), 'wide', scatter_di...  146 us
    psum x1, waiting for transfers between devices, on_device(): modul_all = lax.psum(padded, ('wide', 'narrow'))  126 us
    all_gather x2, waiting for transfers between devices, fetch_rows(): lax.all_gather(weight_tiles[2], 'wide', axis=0, tiled=True)  125 us
    reduce_scatter x2, waiting for transfers between devices, backward_block(): lax.psum_scatter(grad_out_weight.astype(jnp.bfloat16), 'wide', scatter_di...  120 us
  transfers between devices with their start and end apart: 33, of which 28 were waited for; matrix products, arithmetic and copies ran while one was open for 10% of the time, Pallas kernels for 0%

commit v1 on v0

v1 whole, which is shorter than its diff:
```python
import functools

import jax
import jax.numpy as jnp
from jax import lax
from jax.experimental import pallas as pl
from jax.experimental.pallas import tpu as pltpu
from jax.sharding import PartitionSpec as P

HEAD_DIM = 72
PATCHES = 256
CLIP_LEN = 16
STEP = 10
KINDS = 12


HIGHEST_PREC = lax.Precision.HIGHEST
NORM_EPS = 1e-06
BETA_ONE = 0.9
BETA_TWO = 0.999
ADAM_EPS = 1e-06
WEIGHT_DECAY = 0.01
LEARN_RATE = 0.5
CLIP_LIMIT = 1.0
MASKED = -1e30
MESH = pl.DeviceIdType.MESH
BF16 = jnp.bfloat16
F32 = jnp.float32


def greet(partners):
    barrier = pltpu.get_barrier_semaphore()
    count = 0
    for wide_to, narrow_to, cond in partners:

        def send(wide_to=wide_to, narrow_to=narrow_to):
            pl.semaphore_signal(
                barrier, inc=1, device_id=(wide_to, narrow_to), device_id_type=MESH
            )

        if cond is None:
            send()
            count = count + 1
        else:
            pl.when(cond)(send)
            count = count + jnp.where(cond, 1, 0)
    pl.semaphore_wait(barrier, count)


def begin_swaps(groups, narrow_count, sources, targets, local_sem, send_sem, recv_sem, others=()):
    total = len(groups)
    wide_at, narrow_at = lax.axis_index("wide"), lax.axis_index("narrow")
    half = wide_at % 2

    def member(size, index):
        if size == narrow_count:
            return wide_at, index
        return wide_at - half + index // narrow_count, index % narrow_count

    largest = max(groups)
    me_of = {narrow_count: narrow_at, 2 * narrow_count: half * narrow_count + narrow_at}

    def keep(at):
        me = me_of[groups[at]]
        return pltpu.make_async_copy(sources[at].at[me], targets[at].at[me], local_sem.at[at])

    def exchange(at, step, out_at, in_at, to):
        return pltpu.make_async_remote_copy(
            src_ref=sources[at].at[out_at],
            dst_ref=targets[at].at[in_at],
            send_sem=send_sem.at[at, step],
            recv_sem=recv_sem.at[at, step],
            device_id=member(groups[at], to),
            device_id_type=MESH,
        )

    def each():
        for step in range(1, largest):
            for at in range(total):
                if step < groups[at]:
                    yield at, step, groups[at], me_of[groups[at]]

    for at in range(total):
        keep(at).start()
    greet(
        [
            member(largest, (me_of[largest] + step) % largest) + (None,)
            for step in range(1, largest)
        ]
        + list(others)
    )
    for at, step, size, me in each():
        there = (me + step) % size
        exchange(at, step, there, me, there).start()

    def finish():
        for at in range(total):
            keep(at).wait()
        for at, step, size, me in each():
            there = (me + step) % size
            exchange(at, step, there, me, there).wait_send()
            origin = (me + size - step) % size
            exchange(at, step, origin, origin, origin).wait_recv()

    return finish


def swap_kernel(groups, narrow_count, *refs):
    total = len(groups)
    begin_swaps(groups, narrow_count, refs[:total], refs[total : 2 * total], *refs[2 * total :])()


def swap(arrays, collective_id, name):
    narrow_count = lax.axis_size("narrow")
    groups = tuple(a.shape[0] for a in arrays)
    total = len(arrays)
    largest = max(groups)
    return pl.pallas_call(
        functools.partial(swap_kernel, groups, narrow_count),
        out_shape=[jax.ShapeDtypeStruct(a.shape, a.dtype) for a in arrays],
        in_specs=[pl.BlockSpec(memory_space=pl.ANY)] * total,
        out_specs=[pl.BlockSpec(memory_space=pl.ANY)] * total,
        scratch_shapes=[
            pltpu.SemaphoreType.DMA((total,)),
            pltpu.SemaphoreType.DMA((total, largest)),
            pltpu.SemaphoreType.DMA((total, largest)),
        ],
        compiler_params=pltpu.CompilerParams(
            collective_id=collective_id, has_side_effects=True
        ),
        name=name,
    )(*arrays)


def places():
    wide_at, narrow_at = lax.axis_index("wide"), lax.axis_index("narrow")
    x_at, z_at = wide_at % 2, wide_at // 2
    core, y_at = narrow_at % 2, narrow_at // 2
    flip_x, flip_y = 1 - 2 * x_at, 2 - 4 * y_at
    first = (wide_at + (1 - core) * flip_x, narrow_at + core * flip_y)
    second = (wide_at + core * flip_x, narrow_at + (1 - core) * flip_y)
    sibling = (wide_at, narrow_at + 1 - 2 * core)
    return wide_at, narrow_at, x_at, z_at, first, second, sibling


def gather_kernel(layers, lines, own_ref, *refs):
    fulls = refs[:layers]
    local_sem, zs_sem, zr_sem, ps_sem, pr_sem = refs[layers:]
    wide_at, narrow_at, x_at, z_at, first, second, sibling = places()
    chunks = [(layer, j) for layer in range(layers) for j in range(3)]

    def own_block(q):
        layer, j = chunks[q]
        return pltpu.make_async_copy(
            own_ref.at[layer, j],
            fulls[layer].at[3 * narrow_at + j, z_at, x_at],
            local_sem.at[q],
        )

    for q in range(len(chunks)):
        own_block(q).start()
    up_ok, down_ok = z_at + 1 < lines, z_at >= 1
    greet(
        [
            (wide_at + 2, narrow_at, up_ok),
            (wide_at - 2, narrow_at, down_ok),
            first + (None,),
            second + (None,),
            sibling + (None,),
        ]
    )

    def hop(q, up, h, origin):
        layer, j = chunks[q]
        block = fulls[layer].at[3 * narrow_at + j, origin, x_at]
        return pltpu.make_async_remote_copy(
            src_ref=block,
            dst_ref=block,
            send_sem=zs_sem.at[q, up, h],
            recv_sem=zr_sem.at[q, up, h],
            device_id=(wide_at + (2 if up else -2), narrow_at),
            device_id_type=MESH,
        )

    def hop_sends(q, h, act):
        pl.when(jnp.logical_and(up_ok, z_at - h >= 0))(
            lambda: act(hop(q, 1, h, z_at - h))
        )
        pl.when(jnp.logical_and(down_ok, z_at + h < lines))(
            lambda: act(hop(q, 0, h, z_at + h))
        )

    def hop_receives(q, h):
        pl.when(z_at - 1 - h >= 0)(lambda: hop(q, 1, h, z_at - 1 - h).wait_recv())
        pl.when(z_at + 1 + h < lines)(lambda: hop(q, 0, h, z_at + 1 + h).wait_recv())

    def plane(q, slot, narrow_of, x_of, partner):
        layer, j = chunks[q]
        column = fulls[layer].at[3 * narrow_of + j, :, x_of]
        return pltpu.make_async_remote_copy(
            src_ref=column,
            dst_ref=column,
            send_sem=ps_sem.at[q, slot],
            recv_sem=pr_sem.at[q, slot],
            device_id=partner,
            device_id_type=MESH,
        )

    me = (narrow_at, x_at)
    one = (first[1], first[0] % 2)
    two = (second[1], second[0] % 2)
    both = (first[1] + second[1] - narrow_at, 1 - x_at)
    sends = [
        (me, first),
        (me, second),
        (one, second),
        (me, sibling),
        (one, sibling),
        (two, sibling),
        (both, sibling),
    ]
    over = sibling[1] - narrow_at
    arrivals = [
        one,
        two,
        both,
        (me[0] + over, me[1]),
        (one[0] + over, one[1]),
        (two[0] + over, two[1]),
        (both[0] + over, both[1]),
    ]

    def send(q, slot):
        plane(q, slot, *sends[slot][0], sends[slot][1]).start()

    def receive(q, slot):
        plane(q, slot, *arrivals[slot], sends[slot][1]).wait_recv()

    stages = lines + 3

    def stage(q, s):
        if s == 0:
            own_block(q).wait()
            if lines > 1:
                hop_sends(q, 0, lambda copy: copy.start())
        elif s < lines - 1:
            hop_receives(q, s - 1)
            hop_sends(q, s, lambda copy: copy.start())
        elif s == lines - 1:
            hop_receives(q, s - 1)
        if s == lines - 1:
            send(q, 0)
            send(q, 1)
            send(q, 3)
        if s == lines:
            receive(q, 0)
            send(q, 2)
            send(q, 4)
        if s == lines + 1:
            receive(q, 1)
            send(q, 5)
            receive(q, 2)
            send(q, 6)
        if s == lines + 2:
            for slot in range(3, 7):
                receive(q, slot)

    for t in range(len(chunks) + stages - 1):
        for q in range(len(chunks)):
            if 0 <= t - q < stages:
                stage(q, t - q)
    for q in range(len(chunks)):
        for h in range(lines - 1):
            hop_sends(q, h, lambda copy: copy.wait_send())
        for slot in range(7):
            plane(q, slot, *sends[slot][0], sends[slot][1]).wait_send()


def gather_weights(own, collective_id):
    layers, per, rows, width = own.shape
    wide_count = lax.axis_size("wide")
    lines = wide_count // 2
    chunks = layers * per
    fulls = pl.pallas_call(
        functools.partial(gather_kernel, layers, lines),
        out_shape=[
            jax.ShapeDtypeStruct((KINDS, lines, 2, rows, width), own.dtype)
            for _ in range(layers)
        ],
        in_specs=[pl.BlockSpec(memory_space=pl.ANY)],
        out_specs=[pl.BlockSpec(memory_space=pl.ANY)] * layers,
        scratch_shapes=[
            pltpu.SemaphoreType.DMA((chunks,)),
            pltpu.SemaphoreType.DMA((chunks, 2, max(lines - 1, 1))),
            pltpu.SemaphoreType.DMA((chunks, 2, max(lines - 1, 1))),
            pltpu.SemaphoreType.DMA((chunks, 7)),
            pltpu.SemaphoreType.DMA((chunks, 7)),
        ],
        compiler_params=pltpu.CompilerParams(
            collective_id=collective_id, has_side_effects=True
        ),
        cost_estimate=pl.CostEstimate(
            flops=0, bytes_accessed=900_000_000, transcendentals=0
        ),
        name="gather_weights",
    )(own)
    return [full.reshape(KINDS, wide_count * rows, width) for full in fulls]


def scatter_kernel(lines, rows, swaps, swap_groups, narrow_count, *refs):
    layers = 2
    chunks = 3 * layers
    acts = [refs[8 * layer : 8 * layer + 8] for layer in range(layers)]
    at = 8 * layers
    swap_from = refs[at : at + swaps]
    out_ref = refs[at + swaps]
    swap_to = refs[at + swaps + 1 : at + 2 * swaps + 1]
    (
        in_a,
        in_b,
        grads,
        from_core,
        from_second,
        from_first,
        from_line,
        pieces,
        in_sem,
        s1,
        r1,
        s2,
        r2,
        s3,
        r3,
        zs,
        zr,
        fs,
        fr,
        swap_local,
        swap_send,
        swap_recv,
        free_core,
        free_second,
        free_first,
        free_line,
    ) = refs[at + 2 * swaps + 1 :]
    wide_at, narrow_at, x_at, z_at, first, second, sibling = places()
    core = narrow_at % 2
    width = grads.shape[-1]
    col_width = width // narrow_count
    up_ok, down_ok = z_at + 1 < lines, z_at >= 1
    z_mirror = lines - 1 - z_at

    def operands(q, owner):
        hidden_one, grad_qkv, grad_attn, heads, hidden_two, grad_upper, grad_mlp, active = acts[
            q // 3
        ]
        kind = 3 * owner + q % 3
        if kind < 3:
            return hidden_one, grad_qkv.at[kind]
        if kind == 3:
            return grad_attn, heads
        if kind < 8:
            return hidden_two, grad_upper.at[kind - 4]
        return grad_mlp, active.at[kind - 8]

    def load(q, owner):
        for i in range(chunks):

            def start(i=i):
                left, right = operands(i, owner)
                pltpu.make_async_copy(
                    left, in_a.at[owner % 2], in_sem.at[owner % 2, 0]
                ).start()
                pltpu.make_async_copy(
                    right, in_b.at[owner % 2], in_sem.at[owner % 2, 1]
                ).start()

            pl.when(q == i)(start)

    def loaded(owner):
        left, right = operands(0, owner)
        pltpu.make_async_copy(left, in_a.at[owner % 2], in_sem.at[owner % 2, 0]).wait()
        pltpu.make_async_copy(right, in_b.at[owner % 2], in_sem.at[owner % 2, 1]).wait()

    load(0, 0)
    finish_swaps = begin_swaps(
        swap_groups,
        narrow_count,
        swap_from,
        swap_to,
        swap_local,
        swap_send,
        swap_recv,
        [(wide_at + 2, narrow_at, up_ok), (wide_at - 2, narrow_at, down_ok)],
    )

    def to_core(slot, owner):
        return pltpu.make_async_remote_copy(
            src_ref=grads.at[slot, owner],
            dst_ref=from_core.at[slot, owner // 2],
            send_sem=s1.at[slot, owner // 2],
            recv_sem=r1.at[slot, owner // 2],
            device_id=sibling,
            device_id_type=MESH,
        )

    two = (second[1], second[0] % 2)
    both = (first[1] + second[1] - narrow_at, 1 - x_at)
    one = (first[1], first[0] % 2)

    def to_second(slot, place):
        owner, x_of = (two, both)[place]
        return pltpu.make_async_remote_copy(
            src_ref=grads.at[slot, owner, :, x_of],
            dst_ref=from_second.at[slot, place],
            send_sem=s2.at[slot, place],
            recv_sem=r2.at[slot, place],
            device_id=second,
            device_id_type=MESH,
        )

    def to_first(slot):
        return pltpu.make_async_remote_copy(
            src_ref=from_second.at[slot, 1],
            dst_ref=from_first.at[slot],
            send_sem=s3.at[slot],
            recv_sem=r3.at[slot],
            device_id=first,
            device_id_type=MESH,
        )

    def target(up, s):
        return lines - 1 - s + z_at if up else s - z_mirror

    def to_line(slot, up, s, place):
        return pltpu.make_async_remote_copy(
            src_ref=from_first.at[slot, place],
            dst_ref=from_line.at[slot, up, s],
            send_sem=zs.at[slot, up, s],
            recv_sem=zr.at[slot, up, s],
            device_id=(wide_at + (2 if up else -2), narrow_at),
            device_id_type=MESH,
        )

    def to_owner(q, slot, step):
        there = (narrow_at + step) % narrow_count
        return pltpu.make_async_remote_copy(
            src_ref=pieces.at[slot, there],
            dst_ref=out_ref.at[1 - q // 3, 3 * narrow_at + q % 3],
            send_sem=fs.at[slot, step],
            recv_sem=fr.at[q, step],
            device_id=(wide_at, there),
            device_id_type=MESH,
        )

    def keep_own(q, slot):
        return pltpu.make_async_copy(
            pieces.at[slot, narrow_at],
            out_ref.at[1 - q // 3, 3 * narrow_at + q % 3],
            fs.at[slot, 0],
        )

    def compute(q):
        slot = q % 2
        pl.when(q >= 2)(lambda: pl.semaphore_wait(free_core, 1))
        for owner in range(4):
            if owner < 3:
                load(q, owner + 1)
            else:
                load(q + 1, 0)
            loaded(owner)
            place = owner % 2
            tile = 384 if width % 384 == 0 else width

            def columns(i, carry, owner=owner, place=place, tile=tile):
                cols = pl.ds(pl.multiple_of(i * tile, 128), tile)
                total = lax.dot_general(
                    in_a[place],
                    in_b[place, :, cols],
                    (((0,), (0,)), ((), ())),
                    preferred_element_type=F32,
                ).astype(BF16)
                for z in range(lines):
                    for x in range(2):
                        start = (2 * z + x) * rows
                        grads[slot, owner, z, x, :, cols] = total[start : start + rows]
                return carry

            lax.fori_loop(0, width // tile, columns, 0)
            pl.when(core != owner % 2)(lambda owner=owner: to_core(slot, owner).start())

    def add_core(q):
        slot = q % 2
        for half in range(2):
            to_core(slot, 2 * half).wait_recv()
            mine = 2 * half + core

            def body(z, carry, half=half, mine=mine):
                for x in range(2):
                    grads[slot, mine, z, x] = grads[slot, mine, z, x] + from_core[slot, half, z, x]
                return carry

            lax.fori_loop(0, lines, body, 0)
        for half in range(2):
            to_core(slot, 2 * half + 1).wait_send()
        pl.when(q + 2 < chunks)(
            lambda: pl.semaphore_signal(
                free_core, inc=1, device_id=sibling, device_id_type=MESH
            )
        )
        pl.when(q >= 2)(lambda: pl.semaphore_wait(free_second, 1))
        to_second(slot, 1).start()
        to_second(slot, 0).start()

    def add_second(q):
        slot = q % 2
        for place in (1, 0):
            owner, x_of = ((narrow_at, x_at), one)[place]
            to_second(slot, place).wait_recv()

            def body(z, carry, place=place, owner=owner, x_of=x_of):
                from_second[slot, place, z] = (
                    from_second[slot, place, z] + grads[slot, owner, z, x_of]
                )
                return carry

            lax.fori_loop(0, lines, body, 0)
            if place == 1:
                pl.when(q >= 2)(lambda: pl.semaphore_wait(free_first, 1))
                to_first(slot).start()
        for place in (1, 0):
            to_second(slot, place).wait_send()

    def line_hop(q, s):
        slot = q % 2
        for up in (1, 0):
            here = z_at if up else z_mirror
            place = target(up, s)
            if s >= 1:

                def take(up=up, place=place):
                    to_line(slot, up, s - 1, 0).wait_recv()
                    from_first[slot, place] = from_first[slot, place] + from_line[slot, up, s - 1]

                pl.when(jnp.logical_and(here >= 1, here <= s))(take)
            if s < lines - 1:
                pl.when(here <= s)(
                    lambda up=up, place=place: to_line(slot, up, s, place).start()
                )

    def add_first(q):
        slot = q % 2
        to_first(slot).wait_recv()

        def body(z, carry):
            from_first[slot, z] = from_first[slot, z] + from_second[slot, 0, z]
            return carry

        lax.fori_loop(0, lines, body, 0)
        to_first(slot).wait_send()
        pl.when(q + 2 < chunks)(
            lambda: pl.semaphore_signal(
                free_second, inc=1, device_id=second, device_id_type=MESH
            )
        )
        if lines > 1:
            pl.when(jnp.logical_and(q >= 2, up_ok))(
                lambda: pl.semaphore_wait(free_line.at[1], 1)
            )
            pl.when(jnp.logical_and(q >= 2, down_ok))(
                lambda: pl.semaphore_wait(free_line.at[0], 1)
            )
            line_hop(q, 0)

    def finish(q):
        slot = q % 2
        if lines > 1:
            line_hop(q, lines - 1)
            for s in range(lines - 1):
                pl.when(z_at <= s)(lambda s=s: to_line(slot, 1, s, 0).wait_send())
                pl.when(z_mirror <= s)(lambda s=s: to_line(slot, 0, s, 0).wait_send())
            pl.when(jnp.logical_and(q + 2 < chunks, down_ok))(
                lambda: pl.semaphore_signal(
                    free_line.at[1],
                    inc=1,
                    device_id=(wide_at - 2, narrow_at),
                    device_id_type=MESH,
                )
            )
            pl.when(jnp.logical_and(q + 2 < chunks, up_ok))(
                lambda: pl.semaphore_signal(
                    free_line.at[0],
                    inc=1,
                    device_id=(wide_at + 2, narrow_at),
                    device_id_type=MESH,
                )
            )

        def release(last):
            keep_own(last, last % 2).wait()
            for step in range(1, narrow_count):
                to_owner(last, last % 2, step).wait_send()

        pl.when(q >= 2)(lambda: release(q - 2))
        total = from_first[slot, z_at]
        for there in range(narrow_count):
            pieces[slot, there] = total[:, there * col_width : (there + 1) * col_width]
        pl.when(q + 2 < chunks)(
            lambda: pl.semaphore_signal(
                free_first, inc=1, device_id=first, device_id_type=MESH
            )
        )
        keep_own(q, slot).start()
        for step in range(1, narrow_count):
            to_owner(q, slot, step).start()
        return release

    def iteration(t, carry):
        def when(lag, act):
            q = t - lag
            pl.when(jnp.logical_and(q >= 0, q < chunks))(lambda: act(q))

        when(3, add_first)
        when(1, add_core)
        if lines > 2:
            when(3, lambda q: line_hop(q, 1))
        when(2, add_second)

        def rest(q):
            for s in range(2, lines - 1):
                line_hop(q, s)

        if lines > 3:
            when(3, rest)
        when(0, compute)
        when(3, lambda q: finish(q) and None)
        return carry

    lax.fori_loop(0, chunks + 3, iteration, 0)
    for last in (chunks - 2, chunks - 1):
        keep_own(last, last % 2).wait()
        for step in range(1, narrow_count):
            to_owner(last, last % 2, step).wait_send()

    def arrived(q, carry):
        for step in range(1, narrow_count):
            to_owner(q, 0, step).wait_recv()
        return carry

    lax.fori_loop(0, chunks, arrived, 0)
    finish_swaps()


def scatter_grads(acts, moves, rows, collective_id):
    wide_count, narrow_count = lax.axis_size("wide"), lax.axis_size("narrow")
    lines = wide_count // 2
    tokens, width = acts[0].shape
    col_width = width // narrow_count
    chunks = 6
    swaps = len(moves)
    groups = tuple(a.shape[0] for a in moves)
    largest = max(groups)
    dma = pltpu.SemaphoreType.DMA
    regular = pltpu.SemaphoreType.REGULAR
    block = (lines, 2, rows, width)
    any_spec = pl.BlockSpec(memory_space=pl.ANY)
    results = pl.pallas_call(
        functools.partial(scatter_kernel, lines, rows, swaps, groups, narrow_count),
        out_shape=[jax.ShapeDtypeStruct((2, KINDS, rows, col_width), BF16)]
        + [jax.ShapeDtypeStruct(a.shape, a.dtype) for a in moves],
        in_specs=[any_spec] * (len(acts) + swaps),
        out_specs=[any_spec] * (1 + swaps),
        scratch_shapes=[
            pltpu.VMEM((2, tokens, width), BF16),
            pltpu.VMEM((2, tokens, width), BF16),
            pltpu.VMEM((2, 4) + block, BF16),
            pltpu.VMEM((2, 2) + block, BF16),
            pltpu.VMEM((2, 2, lines, rows, width), BF16),
            pltpu.VMEM((2, lines, rows, width), BF16),
            pltpu.VMEM((2, 2, max(lines - 1, 1), rows, width), BF16),
            pltpu.VMEM((2, narrow_count, rows, col_width), BF16),
            dma((2, 2)),
            dma((2, 2)),
            dma((2, 2)),
            dma((2, 2)),
            dma((2, 2)),
            dma((2,)),
            dma((2,)),
            dma((2, 2, max(lines - 1, 1))),
            dma((2, 2, max(lines - 1, 1))),
            dma((2, narrow_count)),
            dma((chunks, narrow_count)),
            dma((swaps,)),
            dma((swaps, largest)),
            dma((swaps, largest)),
            regular,
            regular,
            regular,
            regular((2,)),
        ],
        compiler_params=pltpu.CompilerParams(
            collective_id=collective_id,
            has_side_effects=True,
            vmem_limit_bytes=61 * 1024 * 1024,
        ),
        cost_estimate=pl.CostEstimate(
            flops=2 * 2 * KINDS * width * width * tokens,
            bytes_accessed=900_000_000,
            transcendentals=0,
        ),
        name="scatter_grads",
    )(*acts, *moves)
    return results[0], results[1:]


def normalize(full_rows):
    row_mean = jnp.mean(full_rows, axis=-1, keepdims=True)
    centered = full_rows - row_mean
    inverse = lax.rsqrt(jnp.mean(centered * centered, axis=-1, keepdims=True) + NORM_EPS)
    return (centered * inverse, inverse)


def norm_modulate(residual, shift_vec, scale_vec):
    normed, inverse = normalize(residual.astype(BF16).astype(F32))
    hidden = (normed * (1.0 + scale_vec) + shift_vec).astype(BF16)
    return (normed, inverse, hidden)


def norm_backward(grad_hidden, normed, inverse, scale_vec):
    grad_normed = grad_hidden * (1.0 + scale_vec)
    row_first = jnp.mean(grad_normed, axis=-1, keepdims=True)
    row_second = jnp.mean(grad_normed * normed, axis=-1, keepdims=True)
    grad_input = inverse * (grad_normed - row_first - normed * row_second)
    return (grad_input, jnp.sum(grad_hidden, axis=0), jnp.sum(grad_hidden * normed, axis=0))


def masked_scores(queries, key_rows, key_mask):
    head_scale = queries.shape[-1] ** (-0.5)
    scores = (
        jnp.einsum("blhe,bmhe->bhlm", queries, key_rows, preferred_element_type=F32) * head_scale
    )
    if key_mask is not None:
        scores = jnp.where(key_mask[None, None], scores, MASKED)
    return (scores, head_scale)


def attend_forward(queries, key_rows, value_rows, key_mask):
    scores, _ = masked_scores(queries, key_rows, key_mask)
    row_max = jnp.max(scores, axis=-1, keepdims=True)
    raised = jnp.exp(scores - row_max)
    summed = jnp.sum(raised, axis=-1, keepdims=True)
    attn_probs = (raised / summed).astype(BF16)
    outputs = jnp.einsum("bhlm,bmhe->blhe", attn_probs, value_rows, preferred_element_type=F32)
    return (outputs.astype(BF16), (row_max, summed))


def attend_backward(queries, key_rows, value_rows, key_mask, softmax_stats, grad_outputs):
    row_max, summed = softmax_stats
    scores, head_scale = masked_scores(queries, key_rows, key_mask)
    attn_probs = jnp.exp(scores - row_max) / summed
    grad_probs = jnp.einsum(
        "blhe,bmhe->bhlm", grad_outputs, value_rows, preferred_element_type=F32
    )
    row_delta = jnp.sum(grad_probs * attn_probs, axis=-1, keepdims=True)
    grad_scores = (attn_probs * (grad_probs - row_delta)).astype(BF16)
    grad_queries = (
        jnp.einsum("bhlm,bmhe->blhe", grad_scores, key_rows, preferred_element_type=F32)
        * head_scale
    ).astype(BF16)
    grad_keys = (
        jnp.einsum("bhlm,blhe->bmhe", grad_scores, queries, preferred_element_type=F32)
        * head_scale
    ).astype(BF16)
    grad_values = jnp.einsum(
        "bhlm,blhe->bmhe", attn_probs.astype(BF16), grad_outputs, preferred_element_type=F32
    ).astype(BF16)
    return (grad_queries, grad_keys, grad_values)


def split_heads(rows, length):
    tokens, width = rows.shape
    return rows.reshape(tokens // length, length, width // HEAD_DIM, HEAD_DIM)


def forward_block(residual, modul, weights, bias_rows, length, key_mask):
    expand = (KINDS - 4)//2
    tokens, width = residual.shape
    normed_one, inverse_one, hidden_one = norm_modulate(residual, modul[0], modul[1])
    qkv_bias = jnp.stack([bias_rows[0], jnp.zeros_like(bias_rows[0]), bias_rows[1]])
    qkv_rows = (
        jnp.einsum("td,kde->kte", hidden_one, weights[0:3], preferred_element_type=F32)
        + qkv_bias[:, None, :]
    ).astype(BF16)
    arranged = [split_heads(qkv_rows[kind], length) for kind in range(3)]
    outputs, softmax_stats = attend_forward(*arranged, key_mask)
    heads_out = outputs.reshape(tokens, width)
    attn_branch = (
        jnp.einsum("te,de->td", heads_out, weights[3], preferred_element_type=F32) + bias_rows[2]
    )
    middle = residual + modul[2] * attn_branch
    normed_two, inverse_two, hidden_two = norm_modulate(middle, modul[3], modul[4])
    upper = (
        jnp.einsum("td,kde->kte", hidden_two, weights[4 : 4 + expand], preferred_element_type=F32)
        + bias_rows[3 : 3 + expand][:, None, :]
    )
    active = jax.nn.gelu(upper, approximate=True).astype(BF16)
    mlp_branch = (
        jnp.einsum("kte,kde->td", active, weights[4 + expand :], preferred_element_type=F32)
        + bias_rows[3 + expand]
    )
    output = middle + modul[5] * mlp_branch
    kept_vals = (
        normed_one,
        inverse_one,
        hidden_one,
        heads_out,
        (arranged, softmax_stats),
        attn_branch,
        normed_two,
        inverse_two,
        hidden_two,
        upper,
        active,
        mlp_branch,
    )
    return (output, kept_vals)


def backward_block(grad_out, kept_vals, modul, weights, length, key_mask):
    (
        normed_one,
        inverse_one,
        hidden_one,
        heads_out,
        kept_attn,
        attn_branch,
        normed_two,
        inverse_two,
        hidden_two,
        upper,
        active,
        mlp_branch,
    ) = kept_vals
    expand = (KINDS - 4)//2
    tokens, width = grad_out.shape
    arranged, softmax_stats = kept_attn
    grad_mlp = (grad_out * modul[5]).astype(BF16)
    grad_gate_two = jnp.sum(grad_out * mlp_branch, axis=0)
    grad_active = jnp.einsum(
        "td,kde->kte", grad_mlp, weights[4 + expand :], preferred_element_type=F32
    )
    gelu_pull = jax.vjp(lambda value_in: jax.nn.gelu(value_in, approximate=True), upper)[1]
    grad_upper = gelu_pull(grad_active)[0].astype(BF16)
    grad_hidden_two = jnp.einsum(
        "kte,kde->td", grad_upper, weights[4 : 4 + expand], preferred_element_type=F32
    )
    grad_norm_two, grad_shift_two, grad_scale_two = norm_backward(
        grad_hidden_two, normed_two, inverse_two, modul[4]
    )
    grad_middle = grad_out + grad_norm_two
    grad_attn = (grad_middle * modul[2]).astype(BF16)
    grad_gate_one = jnp.sum(grad_middle * attn_branch, axis=0)
    grad_heads = jnp.einsum(
        "td,de->te", grad_attn, weights[3], preferred_element_type=F32
    ).astype(BF16)
    grad_parts = attend_backward(
        *arranged, key_mask, softmax_stats, split_heads(grad_heads, length)
    )
    grad_qkv = jnp.stack([part.reshape(tokens, width) for part in grad_parts])
    grad_hidden_one = jnp.einsum(
        "kte,kde->td", grad_qkv, weights[0:3], preferred_element_type=F32
    )
    grad_norm_one, grad_shift_one, grad_scale_one = norm_backward(
        grad_hidden_one, normed_one, inverse_one, modul[1]
    )
    grad_input = grad_middle + grad_norm_one
    operands = (
        hidden_one,
        grad_qkv,
        grad_attn,
        heads_out,
        hidden_two,
        grad_upper,
        grad_mlp,
        active,
    )
    grad_modul = jnp.stack(
        [
            grad_shift_one,
            grad_scale_one,
            grad_gate_one,
            grad_shift_two,
            grad_scale_two,
            grad_gate_two,
        ]
    )
    qkv_sums = jnp.sum(grad_qkv, axis=1, dtype=F32)
    grad_lin = jnp.concatenate(
        [
            qkv_sums[0:1],
            qkv_sums[2:3],
            jnp.sum(grad_attn, axis=0, dtype=F32)[None],
            jnp.sum(grad_upper, axis=1, dtype=F32),
            jnp.sum(grad_mlp, axis=0, dtype=F32)[None],
        ],
        axis=0,
    )
    return (grad_input, grad_modul, grad_lin, operands)


def on_device(
    block_input,
    condition,
    frame_counts,
    cotangent,
    qkv_weight,
    qkv_first,
    qkv_second,
    out_weight,
    out_first,
    out_second,
    up_weight,
    up_first,
    up_second,
    down_weight,
    down_first,
    down_second,
    ada_weight,
    ada_first,
    ada_second,
    bias_weight,
    bias_first,
    bias_second,
):
    wide_count = lax.axis_size("wide")
    narrow_count = lax.axis_size("narrow")
    wide_at = lax.axis_index("wide")
    narrow_at = lax.axis_index("narrow")
    frames = block_input.shape[0] // PATCHES
    clip_total = condition.shape[0]
    col_width = block_input.shape[1]
    rows_tile = qkv_weight.shape[1]
    expand = up_weight.shape[2]
    full_width = col_width * narrow_count
    col_start = narrow_at * col_width
    clip_devices = 2 * narrow_count
    own_frames = frames // narrow_count
    own_patches = PATCHES // clip_devices
    own_tokens = own_frames * PATCHES
    clip_at = wide_at // 2

    silu_cond = jax.nn.silu(condition)
    cond_rows = lax.dynamic_slice_in_dim(silu_cond, wide_at * rows_tile, rows_tile, 1)
    partial_mod = jnp.einsum("cd,ldke->lcke", cond_rows, ada_weight, precision=HIGHEST_PREC)
    ada_bias = bias_weight[:, 4 + expand : 10 + expand]
    here = (wide_at == 0).astype(F32)
    partial_mod = partial_mod + here * ada_bias[:, None]
    lin_rows = 4 + expand
    packed = jnp.concatenate(
        [
            partial_mod.reshape(2, clip_total * 6, col_width),
            here * bias_weight[:, :lin_rows],
        ],
        axis=1,
    )
    zero_at = jnp.zeros((), jnp.int32)
    padded = lax.dynamic_update_slice(
        jnp.zeros((2, clip_total * 6 + lin_rows, full_width), F32),
        packed,
        (zero_at, zero_at, col_start),
    )
    vectors = lax.psum(padded, ("wide", "narrow"))
    modul = lax.dynamic_slice_in_dim(vectors, clip_at * 6, 6, 1)
    lin_bias = vectors[:, clip_total * 6 :]

    tiles = jnp.concatenate(
        [
            jnp.transpose(qkv_weight.astype(BF16), (0, 2, 1, 3)),
            out_weight.astype(BF16)[:, None],
            jnp.transpose(up_weight.astype(BF16), (0, 2, 1, 3)),
            jnp.transpose(down_weight.astype(BF16), (0, 2, 1, 3)),
        ],
        axis=1,
    )
    per = KINDS // narrow_count
    tiles = jnp.transpose(
        tiles.reshape(2, narrow_count, per, rows_tile, col_width), (1, 0, 2, 3, 4)
    )
    inputs_by_frame = block_input.astype(BF16).reshape(narrow_count, own_tokens, col_width)
    cot_by_patch = jnp.transpose(
        cotangent.astype(BF16).reshape(frames, clip_devices, own_patches, col_width), (1, 0, 2, 3)
    )
    tiles, inputs_by_frame, cot_by_patch = swap((tiles, inputs_by_frame, cot_by_patch), 0, "swap_in")
    own = jnp.transpose(tiles, (1, 2, 3, 0, 4)).reshape(2, per, rows_tile, full_width)
    weights = gather_weights(own, 1)

    residual = (
        jnp.transpose(inputs_by_frame, (1, 0, 2)).reshape(own_tokens, full_width).astype(F32)
    )
    grad_state = (
        jnp.transpose(
            cot_by_patch.reshape(2, narrow_count, frames, own_patches, col_width), (3, 0, 2, 1, 4)
        )
        .reshape(own_tokens, full_width)
        .astype(F32)
    )

    group = 128
    own_count = lax.dynamic_slice_in_dim(frame_counts, clip_at, 1, 0)[0]
    places_in = jnp.arange(group, dtype=jnp.int32)
    temporal_mask = jnp.logical_and(
        places_in[:, None] // CLIP_LEN == places_in[None, :] // CLIP_LEN,
        (places_in % CLIP_LEN < own_count)[None, :],
    )

    state, kept_spatial = forward_block(
        residual, modul[0], weights[0], lin_bias[0], PATCHES, None
    )
    by_patch = jnp.transpose(
        state.astype(BF16).reshape(own_frames, clip_devices, own_patches, full_width), (1, 0, 2, 3)
    )
    (by_patch,) = swap((by_patch,), 2, "swap_to_patches")
    state = (
        jnp.transpose(by_patch, (2, 0, 1, 3)).reshape(own_tokens, full_width).astype(F32)
    )
    state, kept_temporal = forward_block(
        state, modul[1], weights[1], lin_bias[1], group, temporal_mask
    )
    out_pieces = jnp.transpose(
        state.astype(BF16).reshape(own_patches, 2, frames, narrow_count, col_width),
        (1, 3, 2, 0, 4),
    ).reshape(clip_devices, frames, own_patches, col_width)

    grad_state, grad_modul_t, grad_lin_t, grads_t = backward_block(
        grad_state, kept_temporal, modul[1], weights[1], group, temporal_mask
    )
    by_frame = jnp.transpose(
        grad_state.astype(BF16).reshape(own_patches, clip_devices, own_frames, full_width),
        (1, 2, 0, 3),
    )
    (by_frame,) = swap((by_frame,), 3, "swap_to_frames")
    grad_state = (
        jnp.transpose(by_frame, (1, 0, 2, 3)).reshape(own_tokens, full_width).astype(F32)
    )
    grad_state, grad_modul_s, grad_lin_s, grads_s = backward_block(
        grad_state, kept_spatial, modul[0], weights[0], PATCHES, None
    )
    in_pieces = jnp.transpose(
        grad_state.astype(BF16).reshape(own_tokens, narrow_count, col_width), (1, 0, 2)
    )
    tile_grads, (out_pieces, in_pieces) = scatter_grads(
        grads_t + grads_s, (out_pieces, in_pieces), rows_tile, 4
    )
    block_output = (
        jnp.transpose(out_pieces, (1, 0, 2, 3)).astype(F32).reshape(frames * PATCHES, col_width)
    )
    input_grad = in_pieces.astype(F32).reshape(frames * PATCHES, col_width)

    tile_grads = tile_grads.astype(F32)
    vector_grads = jnp.concatenate(
        [
            lax.dynamic_update_slice(
                jnp.zeros((2, clip_total * 6, full_width), F32),
                jnp.stack([grad_modul_s, grad_modul_t]),
                (zero_at, clip_at * 6, zero_at),
            ),
            jnp.stack([grad_lin_s, grad_lin_t]),
        ],
        axis=1,
    )
    vector_grads = lax.dynamic_slice_in_dim(
        lax.psum(vector_grads, ("wide", "narrow")), col_start, col_width, 2
    )
    grad_clip_mod = vector_grads[:, : clip_total * 6].reshape(2, clip_total, 6, col_width)
    grad_lin = vector_grads[:, clip_total * 6 :]

    grad_ada = jnp.einsum("cd,lcke->ldke", cond_rows, grad_clip_mod, precision=HIGHEST_PREC)
    grad_bias = jnp.concatenate([grad_lin, jnp.sum(grad_clip_mod, axis=1)], axis=1)
    by_rows = lambda part: jnp.transpose(part, (0, 2, 1, 3))
    gradients = (
        by_rows(tile_grads[:, 0:3]),
        tile_grads[:, 3],
        by_rows(tile_grads[:, 4 : 4 + expand]),
        by_rows(tile_grads[:, 4 + expand :]),
        grad_ada,
        grad_bias,
    )
    masters = (qkv_weight, out_weight, up_weight, down_weight, ada_weight, bias_weight)
    firsts = (qkv_first, out_first, up_first, down_first, ada_first, bias_first)
    seconds = (qkv_second, out_second, up_second, down_second, ada_second, bias_second)
    shares = (1.0, 1.0, 1.0, 1.0, 1.0, 1.0 / wide_count)
    local_sq = jnp.zeros((), F32)
    for gradient, share_of in zip(gradients, shares):
        local_sq = local_sq + jnp.sum(gradient * gradient) * share_of
    grad_norm = jnp.sqrt(lax.psum(local_sq, ("wide", "narrow")))
    factor = jnp.minimum(1.0, CLIP_LIMIT / grad_norm)
    first_fix = 1.0 - BETA_ONE**STEP
    second_fix = 1.0 - BETA_TWO**STEP
    updates = []
    states = []
    norm_terms = []
    for master, first_in, second_in, gradient, share_of in zip(
        masters, firsts, seconds, gradients, shares
    ):
        clipped = gradient * factor
        moment = BETA_ONE * first_in + (1.0 - BETA_ONE) * clipped
        square = BETA_TWO * second_in + (1.0 - BETA_TWO) * clipped * clipped
        update = (
            moment / first_fix / (jnp.sqrt(square / second_fix) + ADAM_EPS) + WEIGHT_DECAY * master
        )
        updates.append(update)
        states.append((moment, square))
        norm_terms.append(
            jnp.stack(
                [
                    jnp.sum((master * master).reshape(2, -1), axis=1),
                    jnp.sum((update * update).reshape(2, -1), axis=1),
                ],
                axis=1,
            )
            * share_of
        )
    trust_norms = jnp.sqrt(lax.psum(jnp.stack(norm_terms, axis=1), ("wide", "narrow")))
    trust_ratio = trust_norms[:, :, 0] / trust_norms[:, :, 1]
    results = []
    for position in range(6):
        master = masters[position]
        ratio_here = trust_ratio[:, position].reshape((2,) + (1,) * (master.ndim - 1))
        results.append(master - LEARN_RATE * ratio_here * updates[position])
        results.extend(states[position])
    return (block_output, input_grad, *results, trust_norms, grad_norm.reshape(1))


def solution(mesh):
    tokens = P("wide", "narrow")
    tall = P(None, "wide", None, "narrow")
    flat = P(None, "wide", "narrow")
    bias = P(None, None, "narrow")
    params = (tall,) * 3 + (flat,) * 3 + (tall,) * 9 + (bias,) * 3
    return jax.shard_map(
        on_device,
        mesh=mesh,
        in_specs=(tokens, P(), P(), tokens) + params,
        out_specs=(tokens, tokens) + params + (P(), P()),
        check_vma=False,
    )
```

time: 2680 us -> 1530 us (0.57)
  waiting for transfers between devices: 1550 us -> 115 us
  Pallas kernels: 0 us -> 755 us
  blocking collectives: 411 us -> 81.8 us
  other arithmetic: 192 us -> 105 us
  matrix products: 276 us -> 194 us
  local copies, waits for them, and re-layouts: 205 us -> 252 us
    reduce_scatter x16 -> x0, waiting for transfers between devices: 813 us -> none  [the longest x4 179 us: sum_columns(): lax.psum_scatter(partial_sum.astype(jnp.bfloat16), 'narrow', scatter_dime...]
    pallas_call x0 -> x5, Pallas kernels: none -> 755 us  [the longest x1 343 us: scatter_grads(): pl.pallas_call(functools.partial(scatter_kernel, lines, rows, swaps, grou...]
    all_gather x14 -> x0, waiting for transfers between devices: 506 us -> none  [the longest x8 210 us: whole_rows(): return lax.all_gather(fragment, 'narrow', axis=2, tiled=True)]
    all_to_all x2 -> x0, blocking collectives: 151 us -> none  [the longest x1 108 us: to_frames(): lax.all_to_all(stacked, 'wide', split_axis=1, concat_axis=2, tiled=True)]
    all_to_all x2 -> x0, waiting for transfers between devices: 102 us -> none  [the longest x1 102 us: to_patches(): lax.all_to_all(stacked, 'wide', split_axis=2, concat_axis=1, tiled=True)]
    all_gather x2 -> x0, blocking collectives: 97.8 us -> none  [fetch_rows(): lax.all_gather(weight_tiles[1], 'wide', axis=0, tiled=True)]
    psum x5 -> x0, blocking collectives: 83.6 us -> none  [the longest x4 45.3 us: norm_backward(): lax.psum((jnp.sum(grad_normed, axis=-1, keepdims=True), jnp.sum(grad_norm...]
    dot_general x28 -> x20, matrix products: 234 us -> 171 us  [the longest x2 31.3 us: backward_block(): jnp.einsum('td,kde->kte', grad_mlp, weights[4 + expand:], preferred_eleme...]
  transfers between devices with their start and end apart: 33 -> 2, of which waited for: 28 -> 1; matrix products, arithmetic and copies ran while one was open for 10% -> 7% of each run, Pallas kernels for 0% -> 25%
where the time goes in v1:
time: 1530 us; the launch traced here: 1520 us
  Pallas kernels  755 us (49%)
  local copies, waits for them, and re-layouts  252 us (16%)
  matrix products  194 us (13%)
  waiting for transfers between devices  115 us (8%)
  other arithmetic  105 us (7%)
  blocking collectives  81.8 us (5%)
  between operations  22.4 us (1%)
    pallas_call x1, Pallas kernels, scatter_grads(): pl.pallas_call(functools.partial(scatter_kernel, lines, rows, swaps, grou...  343 us
    pallas_call x1, Pallas kernels, gather_weights(): pl.pallas_call(functools.partial(gather_kernel, layers, lines), out_shape...  311 us
    psum x1, waiting for transfers between devices, on_device(): lax.psum(vector_grads, ('wide', 'narrow'))  115 us
    pallas_call x3, Pallas kernels, swap(): pl.pallas_call(functools.partial(swap_kernel, groups, narrow_count), out_...  100 us
    unnamed x325, local copies, waits for them, and re-layouts  44.9 us
    another operation x14, local copies, waits for them, and re-layouts, backward_block(): grad_qkv = jnp.stack([part.reshape(tokens, width) for part in grad_parts])  43.9 us
    psum x1, blocking collectives, on_device(): grad_norm = jnp.sqrt(lax.psum(local_sq, ('wide', 'narrow')))  41.4 us
    psum x1, blocking collectives, on_device(): lax.psum(jnp.stack(norm_terms, axis=1), ('wide', 'narrow'))  40.4 us
  transfers between devices with their start and end apart: 2, of which 1 were waited for; matrix products, arithmetic and copies ran while one was open for 7% of the time, Pallas kernels for 25%

profile of v1, /device:TPU:0, one launch (start us, length us, event | category | flops | bytes accessed | tf_op | source)
XLA Modules:
  0.0 1524.3 jit_solution(890771507071938393)
XLA Ops:
  29.6 68.4 %swap_in.1 = (bf16[4,2,3,144,288]{4,3,2,1,0:T(8,128)(2,1)}, bf16[4,512,288]{2,1,0:T(8,128)(2,1)}, bf16[8,8,32,288]{3,2,1,0:T(8,128)(2,1)}) custom-call(bf16[4,2,3,144,288]{4,3,2,1,0:T(8,128)(2,1)} %bitcast.374, bf16[4,512,288]{2,1,0:T(8,128)(2,1)} %bitcast.383, bf16[8,8,32,288]{3,2,1,0:T(8,128)(2,1)} %bitcast.381), custom_call_target="tpu_custom_call" | custom-call | tf_op jit(solution)/shard_map/swap_in/pallas_call | solution.py:118
  105.6 5.3 reshape.618.own_ref
  111.0 311.2 %gather_weights.1 = (bf16[12,4,2,144,1152]{4,3,2,1,0:T(8,128)(2,1)}, bf16[12,4,2,144,1152]{4,3,2,1,0:T(8,128)(2,1)}) custom-call(bf16[2,3,144,1152]{3,2,1,0:T(8,128)(2,1)} %reshape.618.own_ref), custom_call_target="tpu_custom_call" | custom-call | bytes 900000000 | tf_op jit(solution)/shard_map/gather_weights/pallas_call | solution.py:284
  425.6 7.0 slice.268
  432.6 15.3 %fusion.169 = (bf16[4,4,2,144,1152]{4,3,2,1,0:T(8,128)(2,1)}, bf16[4,4,2,144,1152]{4,3,2,1,0:T(8,128)(2,1)}) fusion(bf16[12,4,2,144,1152]{4,3,2,1,0:T(8,128)(2,1)} %get-tuple-element.32), kind=kLoop, calls=%fused_computation.368 | loop fusion | bytes 42467328 | tf_op jit(solution)/shard_map/slice | solution.py:808
  451.3 7.0 slice.292
  458.4 15.1 fusion.168
  484.1 3.7 copy.546
  487.8 4.4 reshape.636
  500.3 8.5 fusion.28
  516.5 6.3 fusion.174
  529.3 5.2 convert_reduce_fusion.7
  538.1 10.4 fusion.23
  548.6 10.7 add_convert_fusion.8
  561.7 15.4 %swap_to_patches.1 = bf16[8,2,32,1152]{3,2,1,0:T(8,128)(2,1)} custom-call(bf16[8,2,32,1152]{3,2,1,0:T(8,128)(2,1)} %bitcast.390), custom_call_target="tpu_custom_call" | custom-call | tf_op jit(solution)/shard_map/swap_to_patches/pallas_call | solution.py:118
  589.2 3.7 reshape.650
  599.6 4.1 reshape.635
  603.7 8.7 fusion.29
  629.0 15.7 %fusion.19 = (bf16[4,512,1152]{2,1,0:T(8,128)(2,1)}, f32[4,1152,512]{1,2,0:T(8,128)}) fusion(f32[4,1152]{1,0:T(4,128)S(1)} %copy-done.116, bf16[4,1152,1152]{2,1,0:T(8,128)(2,1)} %bitcast.372, bf16[512,1152]{1,0:T(8,128)(2,1)S(1)} %fusion.54.refs_4_), kind=kOutput, calls=%fused_computation.27 | convolution fusion | flops 5459410944 | bytes 25970688 | tf_op jit(solution)/shard_map/td,kde->kte/dot_general | solution.py:803
  644.7 13.8 convert_reduce_fusion
  658.6 14.3 fusion.59
  674.0 15.7 %multiply_reduce_fusion.6 = (f32[1152]{0:T(1024)}, bf16[512,1152]{1,0:T(8,128)(2,1)}, f32[1152]{0:T(1024)}, f32[512,1152]{1,0:T(8,128)}, bf16[512,1152]{1,0:T(8,128)(2,1)}) fusion(f32[512,1152]{1,0:T(8,128)} %reshape.636, f32[1152]{0:T(1024)} %get-tuple-element.152, f32[512,1152]{1,0:T(8,128)} %reshape.635, f32[512,1152]{1,0:T(8,128)} %get-tuple-element.255, ...), kind=kOutput, calls=%fused_computation.135 | convolution fusion | flops 5448202240 | bytes 30706688 | tf_op jit(solution)/shard_map/kte,kde->td/dot_general | solution.py:808
  695.3 4.7 reshape.666
  700.0 4.4 copy.360
  704.3 4.3 fusion.103
  738.9 9.3 multiply_reduce_fusion.8
  752.2 16.5 %swap_to_frames.1 = bf16[8,2,32,1152]{3,2,1,0:T(8,128)(2,1)} custom-call(bf16[8,2,32,1152]{3,2,1,0:T(8,128)(2,1)} %bitcast.391), custom_call_target="tpu_custom_call" | custom-call | tf_op jit(solution)/shard_map/swap_to_frames/pallas_call | solution.py:118
  771.7 17.4 %convert_reduce_fusion.1 = (f32[4,1152]{1,0:T(4,128)}, bf16[4,512,1152]{2,1,0:T(8,128)(2,1)}) fusion(f32[4,1152,512]{1,2,0:T(8,128)} %get-tuple-element.250, f32[4,1152]{1,0:T(4,128)S(1)} %copy-done.114, bf16[512,1152,1]{1,0,2:T(8,128)(2,1)S(1)} %bitcast.400, bf16[4,1152,1152]{2,1,0:T(8,128)(2,1)} %bitcast.364), kind=kOutput, calls=%fused_computation.35 | convolution fusion | flops 5490077184 | bytes 25989120 | tf_op jit(solution)/shard_map/td,kde->kte/dot_general | solution.py:849
  789.2 10.0 fusion.67
  801.6 4.2 fusion.71
  809.6 5.1 reshape.667
  817.7 6.0 fusion.92
  823.6 4.5 multiply_reduce_fusion
  833.2 4.3 copy.447
  837.5 4.6 reshape.665
  842.1 4.3 copy.445
  846.4 4.6 reshape.663
  854.0 4.8 reshape.664
  861.8 11.7 multiply_reduce_fusion.10
  876.2 4.4 reshape.625
  890.1 343.2 %scatter_grads.1 = (bf16[2,12,144,288]{3,2,1,0:T(8,128)(2,1)}, bf16[8,8,32,288]{3,2,1,0:T(8,128)(2,1)}, bf16[4,512,288]{2,1,0:T(8,128)(2,1)}) custom-call(bf16[512,1152]{1,0:T(8,128)(2,1)} %get-tuple-element.223.refs_0_, bf16[3,512,1152]{2,1,0:T(8,128)(2,1)} %copy-done.32, bf16[512,1152]{1,0:T(8,128)(2,1)} %copy-done.57, bf16[512,1152]{1,0:T(8,128)(2,1)} %copy.396.refs_3_, ...), custom_call_target="tpu_custom_call" | custom-call | flops 32614907904 | bytes 900000000 | tf_op jit(solution)/shard_map/scatter_grads/pallas_call | solution.py:667
  1250.3 114.6 %all-reduce.5.cloned.1.call-done = f32[2,32,1152]{2,0,1:T(2,128)} async-done(((f32[2,32,1152]{2,0,1:T(2,128)}), f32[2,32,1152]{2,0,1:T(2,128)}) %all-reduce.5.cloned.1.call-update) | async-done | bytes 294928 | tf_op jit(solution)/shard_map/psum | solution.py:1072
  1366.0 5.2 multiply_reduce_fusion.5
  1376.1 41.4 %psum.30 = f32[]{:T(128)} all-reduce(f32[]{:T(128)S(6)} %add.501), channel_id=1, replica_groups=mesh['wide'=8,'narrow'=4] {'wide','narrow'}, use_global_device_ids=true, to_apply=%region_52.53 | all-reduce | flops 1 | bytes 8 | tf_op jit(solution)/shard_map/psum | solution.py:1095
  1422.1 6.7 multiply_reduce_fusion.4
  1428.9 5.3 multiply_reduce_fusion.26
  1435.6 9.2 multiply_reduce_fusion.18
  1454.0 40.4 %psum.31 = f32[2,6,2]{1,2,0:T(2,128)S(1)} all-reduce(f32[2,6,2]{1,2,0:T(2,128)S(1)} %copy-done.123), channel_id=1, replica_groups=mesh['wide'=8,'narrow'=4] {'wide','narrow'}, use_global_device_ids=true, to_apply=%region_64.65 | all-reduce | flops 24 | bytes 192 | tf_op jit(solution)/shard_map/psum | solution.py:1123
  (527 shorter events, 240.9 us)
Async XLA Ops:
  7.2 8.7 copy-start.3
  7.2 487.4 %all-reduce.3.cloned.1.call-start = ((), (), s32[]{:S(2)}) async-start(), calls=%async_computation | async-start | bytes 589824 | tf_op jit(solution)/shard_map/psum | solution.py:972
  9.5 7.6 copy-start.43
  15.8 1349.1 %all-reduce.5.cloned.1.call-start = ((), (), s32[]{:S(2)}) async-start(), calls=%async_computation.1 | async-start | bytes 589824 | tf_op jit(solution)/shard_map/psum | solution.py:1072
  458.4 15.1 copy-start.139
  496.9 38.1 %copy-start.77 = (f32[1152]{0:T(1024)}, f32[1152]{0:T(1024)S(1)}, u32[]{:S(2)}) copy-start(f32[1152]{0:T(1024)S(1)} %get-tuple-element.157) | copy-start | bytes 13828
  529.1 8.9 slice-start.2
  529.3 8.8 slice-start.3
  529.3 8.8 slice-start.4
  534.5 14.0 copy-start.91
  534.5 14.0 slice-start.8
  535.0 13.5 copy-start.108
  536.1 12.5 copy-start.60
  538.1 10.5 copy-start.113
  538.1 10.5 slice-start.9
  538.1 10.5 slice-start.10
  538.1 10.5 copy-start.93
  538.1 10.5 copy-start.122
  624.6 20.1 %slice-start.11 = ((s8[10616832]{0:T(1024)(128)(4,1)}), s8[4194304]{0:T(1024)(128)(4,1)S(1)}, s32[]{:S(2)}) async-start(s8[10616832]{0:T(1024)(128)(4,1)} %bitcast.369), calls=%async_computation.13 | async-start | bytes 8388608
  627.9 30.6 %copy-start.110 = (f32[512]{0:T(512)}, f32[512]{0:T(512)S(1)}, u32[]{:S(2)}) copy-start(f32[512]{0:T(512)S(1)} %broadcast_multiply_fusion.8) | copy-start | bytes 6148
  628.4 30.2 %copy-start.120 = (f32[512]{0:T(512)}, f32[512]{0:T(512)S(1)}, u32[]{:S(2)}) copy-start(f32[512]{0:T(512)S(1)} %add_rsqrt_fusion) | copy-start | bytes 6148
  628.9 15.7 %copy-start.63 = (bf16[512,1152]{1,0:T(8,128)(2,1)}, bf16[512,1152]{1,0:T(8,128)(2,1)S(1)}, u32[]{:S(2)}) copy-start(bf16[512,1152]{1,0:T(8,128)(2,1)S(1)} %fusion.54.refs_4_) | copy-start | bytes 3538948
  629.0 15.7 %slice-start.12 = ((s8[10616832]{0:T(1024)(128)(4,1)}), s8[4194304]{0:T(1024)(128)(4,1)S(1)}, s32[]{:S(2)}) async-start(s8[10616832]{0:T(1024)(128)(4,1)} %bitcast.369), calls=%async_computation.14 | async-start | bytes 8388608
  629.0 15.7 %slice-start.13 = ((s8[10616832]{0:T(1024)(128)(4,1)}), s8[2228224]{0:T(1024)(128)(4,1)S(1)}, s32[]{:S(2)}) async-start(s8[10616832]{0:T(1024)(128)(4,1)} %bitcast.369), calls=%async_computation.15 | async-start | bytes 4456448
  629.0 15.7 %copy-start.67 = (bf16[512,1152,1]{1,0,2:T(8,128)(2,1)S(1)}, bf16[512,1152,1]{1,0,2:T(8,128)(2,1)}, u32[]{:S(2)}) copy-start(bf16[512,1152,1]{1,0,2:T(8,128)(2,1)} %reshape.650) | copy-start | bytes 3538948
  658.6 14.3 copy-start.140
  736.0 12.3 copy-start.32
  738.9 9.4 copy-start.26
  738.9 9.4 copy-start.79
  771.0 18.2 %slice-start.5 = ((s8[10616832]{0:T(1024)(128)(4,1)}), s8[4194304]{0:T(1024)(128)(4,1)S(1)}, s32[]{:S(2)}) async-start(s8[10616832]{0:T(1024)(128)(4,1)} %bitcast.361), calls=%async_computation.7 | async-start | bytes 8388608
  771.7 17.5 %copy-start.13 = (bf16[512,1152]{1,0:T(8,128)(2,1)S(1)}, bf16[512,1152]{1,0:T(8,128)(2,1)}, u32[]{:S(2)}) copy-start(bf16[512,1152]{1,0:T(8,128)(2,1)} %copy-done.12) | copy-start | bytes 3538948
  771.7 17.5 %slice-start.6 = ((s8[10616832]{0:T(1024)(128)(4,1)}), s8[4194304]{0:T(1024)(128)(4,1)S(1)}, s32[]{:S(2)}) async-start(s8[10616832]{0:T(1024)(128)(4,1)} %bitcast.361), calls=%async_computation.8 | async-start | bytes 8388608
  771.7 17.5 %slice-start.7 = ((s8[10616832]{0:T(1024)(128)(4,1)}), s8[2228224]{0:T(1024)(128)(4,1)S(1)}, s32[]{:S(2)}) async-start(s8[10616832]{0:T(1024)(128)(4,1)} %bitcast.361), calls=%async_computation.9 | async-start | bytes 4456448
  771.7 17.5 %copy-start.78 = (f32[1152]{0:T(1024)S(1)}, f32[1152]{0:T(1024)}, u32[]{:S(2)}) copy-start(f32[1152]{0:T(1024)} %copy-done.77) | copy-start | bytes 13828
  771.7 17.5 %copy-start.92 = (f32[512]{0:T(512)S(1)}, f32[512]{0:T(512)}, u32[]{:S(2)}) copy-start(f32[512]{0:T(512)} %copy-done.91) | copy-start | bytes 6148
  771.7 17.5 %copy-start.109 = (f32[512]{0:T(512)S(1)}, f32[512]{0:T(512)}, u32[]{:S(2)}) copy-start(f32[512]{0:T(512)} %copy-done.108) | copy-start | bytes 6148
  817.7 10.5 slice-start
  861.8 11.7 copy-start.33
  876.2 8.0 copy-start.136
  876.2 8.0 copy-start.135
  876.2 8.0 copy-start.82
  1373.9 44.3 %copy-start.71 = (f32[2,14,288]{2,0,1:T(2,128)S(1)}, f32[2,14,288]{2,0,1:T(2,128)}, u32[]{:S(2)}) copy-start(f32[2,14,288]{2,0,1:T(2,128)} %param.41) | copy-start | bytes 96772
  1374.0 44.3 %copy-start.85 = (f32[2,14,288]{2,0,1:T(2,128)S(1)}, f32[2,14,288]{2,0,1:T(2,128)}, u32[]{:S(2)}) copy-start(f32[2,14,288]{2,0,1:T(2,128)} %param.42) | copy-start | bytes 96772
  1374.0 44.3 %copy-start.86 = (f32[2,14,288]{2,0,1:T(2,128)S(1)}, f32[2,14,288]{2,0,1:T(2,128)}, u32[]{:S(2)}) copy-start(f32[2,14,288]{2,0,1:T(2,128)} %param.43) | copy-start | bytes 96772
  1376.1 46.0 %copy-start.8 = (f32[2,144,6,288]{3,1,2,0:T(8,128)S(1)}, f32[2,144,6,288]{3,1,2,0:T(8,128)}, u32[]{:S(2)}) copy-start(f32[2,144,6,288]{3,1,2,0:T(8,128)} %param.38) | copy-start | bytes 5971972
  1428.9 6.7 copy-start.4
  1428.9 6.7 copy-start.6
  1435.6 9.2 copy-start.137
  (109 other events, 379.5 us)
Sparse Core Ops, SparseCore 0:
  16.0 133.9 all-reduce.2
  1240.9 124.0 all-reduce.4
